TPU v7x, 32 devices: a whole 2x2x4 slice. The times are simulated.
32 devices in a mesh: blk: 8 (over y, x, core), grp: 4 (over z).
Axes of the slice: x: 2, y: 2, z: 4, core: 2. Of those that a mesh axis runs over, the one named last changes fastest.
Arguments:
- hidden_in: bfloat16 [128, 128, 768], P(('blk', 'grp')), may hold values from -6 to 6
- upstream_grad: bfloat16 [128, 128, 768], P(('blk', 'grp')), may hold values from -6 to 6
- query_vectors: bfloat16 [128, 768], P(('blk', 'grp')), may hold values from -0.5 to 0.5
- loss_weight: float32 [128], P(('blk', 'grp')), may hold values from 4 to 16
- positive_ids: int32 [128, 3], P(('blk', 'grp')), may hold values from 0 to 127, as said below
- positive_count: int32 [128], P(('blk', 'grp')), may hold values from 1 to 3
- query_proj: bfloat16 [768, 768], P(('blk', 'grp')), may hold values from -0.21875 to 0.21875
- key_proj: bfloat16 [768, 768], P(('blk', 'grp')), may hold values from -0.21875 to 0.21875
- value_proj: bfloat16 [768, 768], P(('blk', 'grp')), may hold values from -0.21875 to 0.21875
- attn_proj: bfloat16 [768, 768], P(None, ('blk', 'grp')), may hold values from -1.75 to 1.75
- query_bias: bfloat16 [768], P(('blk', 'grp')), may hold values from -3 to 3
- value_bias: bfloat16 [768], P(('blk', 'grp')), may hold values from -3 to 3
- attn_bias: bfloat16 [768], P(('blk', 'grp')), may hold values from -3 to 3
- first_gain: bfloat16 [768], P(('blk', 'grp')), may hold values from 0.25 to 1.75
- first_shift: bfloat16 [768], P(('blk', 'grp')), may hold values from -2 to 2
- inner_proj: bfloat16 [768, 3072], P(('blk', 'grp')), may hold values from -0.21875 to 0.21875
- inner_bias: bfloat16 [3072], P(('blk', 'grp')), may hold values from -3 to 3
- outer_proj: bfloat16 [3072, 768], P(None, ('blk', 'grp')), may hold values from -0.15625 to 0.15625
- outer_bias: bfloat16 [768], P(('blk', 'grp')), may hold values from -3 to 3
- second_gain: bfloat16 [768], P(('blk', 'grp')), may hold values from 0.25 to 1.75
- second_shift: bfloat16 [768], P(('blk', 'grp')), may hold values from -2 to 2
Outputs:
- layer_output: bfloat16 [128, 128, 768], P(('blk', 'grp'))
- hidden_grad: bfloat16 [128, 128, 768], P(('blk', 'grp'))
- query_grad: float32 [128, 768], P(('blk', 'grp'))
- query_loss: float32 [128], P(('blk', 'grp'))
- grad_query_proj: float32 [768, 768], P(('blk', 'grp'))
- grad_key_proj: float32 [768, 768], P(('blk', 'grp'))
- grad_value_proj: float32 [768, 768], P(('blk', 'grp'))
- grad_attn_proj: float32 [768, 768], P(None, ('blk', 'grp'))
- grad_query_bias: float32 [768], P(('blk', 'grp'))
- grad_value_bias: float32 [768], P(('blk', 'grp'))
- grad_attn_bias: float32 [768], P(('blk', 'grp'))
- grad_first_gain: float32 [768], P(('blk', 'grp'))
- grad_first_shift: float32 [768], P(('blk', 'grp'))
- grad_inner_proj: float32 [768, 3072], P(('blk', 'grp'))
- grad_inner_bias: float32 [3072], P(('blk', 'grp'))
- grad_outer_proj: float32 [3072, 768], P(None, ('blk', 'grp'))
- grad_outer_bias: float32 [768], P(('blk', 'grp'))
- grad_second_gain: float32 [768], P(('blk', 'grp'))
- grad_second_shift: float32 [768], P(('blk', 'grp'))
- cls_grad: float32 [128, 768], P(('blk', 'grp'))
Inputs may be any that keep to these rules, and one draw needn't show every extreme that they name: `positive_ids`: each row holds 3 different passage indices; only the first positive_count of them are the query's positives. Every passage index is the first entry of exactly one row.
All inputs are finite; a program needn't handle non-finite values.
Results may differ from a plain program's by a relative error of at most 0.023.
Values may be sent and summed in bfloat16 or wider, within the bound.
A program may use at most 192 MiB of HBM per device.

v0:
```python
import jax
import jax.numpy as jnp
from jax import lax
from jax.sharding import PartitionSpec as P

D = 768
HEADS = 12
HEAD_DIM = 64
LEN = 128


NORM_EPS = 1e-05
NEG_FILL = -1e30


def product(left_side, right_side):
    return jnp.dot(left_side, right_side, preferred_element_type=jnp.float32)


def contract(form_text, first_side, second_side):
    return jnp.einsum(form_text, first_side, second_side, preferred_element_type=jnp.float32)


def norm_forward(resid_sum, gain_vec, shift_vec):
    centered = resid_sum - jnp.mean(resid_sum, axis=-1, keepdims=True)
    inv_dev = lax.rsqrt(jnp.mean(centered * centered, axis=-1, keepdims=True) + NORM_EPS)
    normal_part = centered * inv_dev
    return (normal_part * gain_vec + shift_vec, normal_part, inv_dev)


def norm_backward(out_grad, normal_part, inv_dev, gain_vec):
    scaled_grad = out_grad * gain_vec
    mean_grad = jnp.mean(scaled_grad, axis=-1, keepdims=True)
    mean_cross = jnp.mean(scaled_grad * normal_part, axis=-1, keepdims=True)
    return inv_dev * (scaled_grad - mean_grad - normal_part * mean_cross)


def gelu_exact(pre_act):
    return jax.nn.gelu(pre_act, approximate=False)


def gelu_grad(pre_act, act_grad):
    unused_out, pullback = jax.vjp(gelu_exact, pre_act)
    return pullback(act_grad)[0]


def positive_block(positive_ids, positive_count, span_count):
    slot_live = (
        jnp.arange(positive_ids.shape[1], dtype=jnp.int32)[None, :] < positive_count[:, None]
    )
    passage_index = jnp.arange(span_count, dtype=jnp.int32)
    matches = (positive_ids[:, :, None] == passage_index[None, None, :]) & slot_live[:, :, None]
    return jnp.any(matches, axis=1)


def block_forward(block_in, attn_params, ffn_params):
    (
        query_proj,
        key_proj,
        value_proj,
        attn_proj,
        query_bias,
        value_bias,
        attn_bias,
        first_gain,
        first_shift,
    ) = attn_params
    inner_proj, inner_bias, outer_proj, outer_bias, second_gain, second_shift = ffn_params
    pass_count = block_in.shape[0]
    head_shape = (pass_count, LEN, HEADS, HEAD_DIM)
    tok_rows = block_in.reshape(pass_count * LEN, D)
    queries = ((product(tok_rows, query_proj) + query_bias) * 0.125).astype(jnp.bfloat16)
    keys_low = product(tok_rows, key_proj).astype(jnp.bfloat16)
    values_low = (product(tok_rows, value_proj) + value_bias).astype(jnp.bfloat16)
    scores = contract("bqhd,bkhd->bhqk", queries.reshape(head_shape), keys_low.reshape(head_shape))
    top_score = jnp.max(scores, axis=-1, keepdims=True)
    exp_terms = jnp.exp(scores - top_score)
    totals = jnp.sum(exp_terms, axis=-1, keepdims=True)
    probs_low = (exp_terms / totals).astype(jnp.bfloat16)
    log_norm = top_score + jnp.log(totals)
    context = contract("bhqk,bkhd->bqhd", probs_low, values_low.reshape(head_shape))
    context = context.reshape(pass_count * LEN, D).astype(jnp.bfloat16)
    attn_out = product(context, attn_proj) + attn_bias
    normed, first_normal, first_inv = norm_forward(
        tok_rows.astype(jnp.float32) + attn_out, first_gain, first_shift
    )
    normed_low = normed.astype(jnp.bfloat16)
    inner_pre = product(normed_low, inner_proj) + inner_bias
    activated = gelu_exact(inner_pre).astype(jnp.bfloat16)
    branch = product(activated, outer_proj) + outer_bias
    layer_f32, second_normal, second_inv = norm_forward(normed + branch, second_gain, second_shift)
    kept_state = (
        queries,
        keys_low,
        values_low,
        log_norm,
        context,
        first_normal,
        first_inv,
        normed_low,
        inner_pre,
        activated,
        second_normal,
        second_inv,
    )
    return (layer_f32, kept_state)


def block_backward(block_in, out_grad, kept_state, attn_params, ffn_params):
    (
        query_proj,
        key_proj,
        value_proj,
        attn_proj,
        query_bias,
        value_bias,
        attn_bias,
        first_gain,
        first_shift,
    ) = attn_params
    inner_proj, inner_bias, outer_proj, outer_bias, second_gain, second_shift = ffn_params
    (
        queries,
        keys_low,
        values_low,
        log_norm,
        context,
        first_normal,
        first_inv,
        normed_low,
        inner_pre,
        activated,
        second_normal,
        second_inv,
    ) = kept_state
    pass_count = block_in.shape[0]
    tok_count = pass_count * LEN
    head_shape = (pass_count, LEN, HEADS, HEAD_DIM)
    tok_rows = block_in.reshape(tok_count, D)
    grad_rows = out_grad.reshape(tok_count, D)
    grad_second_gain = jnp.sum(grad_rows * second_normal, axis=0)
    grad_second_shift = jnp.sum(grad_rows, axis=0)
    second_resid = norm_backward(grad_rows, second_normal, second_inv, second_gain)
    branch_grad = second_resid.astype(jnp.bfloat16)
    grad_outer_bias = jnp.sum(branch_grad.astype(jnp.float32), axis=0)
    grad_outer_proj = product(activated.T, branch_grad)
    inner_grad = gelu_grad(inner_pre, product(branch_grad, outer_proj.T)).astype(jnp.bfloat16)
    grad_inner_bias = jnp.sum(inner_grad.astype(jnp.float32), axis=0)
    grad_inner_proj = product(normed_low.T, inner_grad)
    normed_grad = second_resid + product(inner_grad, inner_proj.T)
    grad_first_gain = jnp.sum(normed_grad * first_normal, axis=0)
    grad_first_shift = jnp.sum(normed_grad, axis=0)
    first_resid = norm_backward(normed_grad, first_normal, first_inv, first_gain)
    attn_grad = first_resid.astype(jnp.bfloat16)
    grad_attn_bias = jnp.sum(attn_grad.astype(jnp.float32), axis=0)
    grad_attn_proj = product(context.T, attn_grad)
    context_grad = product(attn_grad, attn_proj.T).astype(jnp.bfloat16).reshape(head_shape)
    query_heads = queries.reshape(head_shape)
    key_heads = keys_low.reshape(head_shape)
    value_heads = values_low.reshape(head_shape)
    scores = contract("bqhd,bkhd->bhqk", query_heads, key_heads)
    prob_full = jnp.exp(scores - log_norm)
    values_grad = contract("bhqk,bqhd->bkhd", prob_full.astype(jnp.bfloat16), context_grad)
    values_grad = values_grad.astype(jnp.bfloat16).reshape(tok_count, D)
    prob_grad = contract("bqhd,bkhd->bhqk", context_grad, value_heads)
    score_grad = (
        prob_full * (prob_grad - jnp.sum(prob_full * prob_grad, axis=-1, keepdims=True))
    ).astype(jnp.bfloat16)
    queries_grad = (
        contract("bhqk,bkhd->bqhd", score_grad, key_heads)
        .astype(jnp.bfloat16)
        .reshape(tok_count, D)
    )
    keys_grad = (
        contract("bhqk,bqhd->bkhd", score_grad, query_heads)
        .astype(jnp.bfloat16)
        .reshape(tok_count, D)
    )
    grad_query_proj = product(tok_rows.T, queries_grad) * 0.125
    grad_query_bias = jnp.sum(queries_grad.astype(jnp.float32), axis=0) * 0.125
    grad_key_proj = product(tok_rows.T, keys_grad)
    grad_value_proj = product(tok_rows.T, values_grad)
    grad_value_bias = jnp.sum(values_grad.astype(jnp.float32), axis=0)
    hidden_grad = (
        first_resid
        + 0.125 * product(queries_grad, query_proj.T)
        + product(keys_grad, key_proj.T)
        + product(values_grad, value_proj.T)
    )
    attn_grads = (
        grad_query_proj,
        grad_key_proj,
        grad_value_proj,
        grad_attn_proj,
        grad_query_bias,
        grad_value_bias,
        grad_attn_bias,
        grad_first_gain,
        grad_first_shift,
    )
    ffn_grads = (
        grad_inner_proj,
        grad_inner_bias,
        grad_outer_proj,
        grad_outer_bias,
        grad_second_gain,
        grad_second_shift,
    )
    return (hidden_grad, attn_grads, ffn_grads)


def local(
    hidden_in,
    upstream_grad,
    query_vectors,
    loss_weight,
    positive_ids,
    positive_count,
    query_proj,
    key_proj,
    value_proj,
    attn_proj,
    query_bias,
    value_bias,
    attn_bias,
    first_gain,
    first_shift,
    inner_proj,
    inner_bias,
    outer_proj,
    outer_bias,
    second_gain,
    second_shift,
):
    attn_params = (
        lax.all_gather(query_proj, ("blk", "grp"), axis=0, tiled=True),
        lax.all_gather(key_proj, ("blk", "grp"), axis=0, tiled=True),
        lax.all_gather(value_proj, ("blk", "grp"), axis=0, tiled=True),
        lax.all_gather(attn_proj, ("blk", "grp"), axis=1, tiled=True),
        lax.all_gather(query_bias, ("blk", "grp"), axis=0, tiled=True),
        lax.all_gather(value_bias, ("blk", "grp"), axis=0, tiled=True),
        lax.all_gather(attn_bias, ("blk", "grp"), axis=0, tiled=True),
        lax.all_gather(first_gain, ("blk", "grp"), axis=0, tiled=True),
        lax.all_gather(first_shift, ("blk", "grp"), axis=0, tiled=True),
    )
    ffn_params = (
        lax.all_gather(inner_proj, ("blk", "grp"), axis=0, tiled=True),
        lax.all_gather(inner_bias, ("blk", "grp"), axis=0, tiled=True),
        lax.all_gather(outer_proj, ("blk", "grp"), axis=1, tiled=True),
        lax.all_gather(outer_bias, ("blk", "grp"), axis=0, tiled=True),
        lax.all_gather(second_gain, ("blk", "grp"), axis=0, tiled=True),
        lax.all_gather(second_shift, ("blk", "grp"), axis=0, tiled=True),
    )
    pass_count = hidden_in.shape[0]
    layer_f32, kept_state = block_forward(hidden_in, attn_params, ffn_params)
    layer_output = layer_f32.astype(jnp.bfloat16).reshape(pass_count, LEN, D)
    cls_local = layer_output[:, 0, :]
    query_count = query_vectors.shape[0]
    lowest = jnp.full((query_count,), NEG_FILL, jnp.float32)
    cls_piece = lax.all_gather(cls_local, ("blk", "grp"), axis=0, tiled=True)
    top_all = lowest
    top_pos = lowest
    scores = contract("qd,pd->qp", query_vectors, cls_piece)
    hit_mask = positive_block(positive_ids, positive_count, cls_piece.shape[0])
    masked = jnp.where(hit_mask, scores, NEG_FILL)
    new_all = jnp.maximum(top_all, jnp.max(scores, axis=1))
    new_pos = jnp.maximum(top_pos, jnp.max(masked, axis=1))
    sum_all = jnp.sum(jnp.exp(scores - new_all[:, None]), axis=1)
    pos_terms = jnp.where(hit_mask, jnp.exp(masked - new_pos[:, None]), 0.0)
    sum_pos = jnp.sum(pos_terms, axis=1)
    top_all, sum_all, top_pos, sum_pos = (new_all, sum_all, new_pos, sum_pos)
    total_all = top_all + jnp.log(sum_all)
    total_pos = top_pos + jnp.log(sum_pos)
    cls_piece = lax.all_gather(cls_local, ("blk", "grp"), axis=0, tiled=True)
    scores = contract("qd,pd->qp", query_vectors, cls_piece)
    hit_mask = positive_block(positive_ids, positive_count, cls_piece.shape[0])
    masked = jnp.where(hit_mask, scores, NEG_FILL)
    weight_rows = loss_weight[:, None] * (
        jnp.exp(scores - total_all[:, None]) - jnp.exp(masked - total_pos[:, None])
    )
    weight_rows = weight_rows.astype(jnp.bfloat16)
    query_acc = product(weight_rows, cls_piece)
    query_loss = total_all - total_pos
    cls_grad = lax.psum_scatter(
        contract("qp,qd->pd", weight_rows, query_vectors),
        ("blk", "grp"),
        scatter_dimension=0,
        tiled=True,
    )
    grad_total = upstream_grad.astype(jnp.float32).at[:, 0, :].add(cls_grad)
    ffn_back = (
        lax.all_gather(inner_proj, ("blk", "grp"), axis=0, tiled=True),
        lax.all_gather(inner_bias, ("blk", "grp"), axis=0, tiled=True),
        lax.all_gather(outer_proj, ("blk", "grp"), axis=1, tiled=True),
        lax.all_gather(outer_bias, ("blk", "grp"), axis=0, tiled=True),
        lax.all_gather(second_gain, ("blk", "grp"), axis=0, tiled=True),
        lax.all_gather(second_shift, ("blk", "grp"), axis=0, tiled=True),
    )
    attn_back = (
        lax.all_gather(query_proj, ("blk", "grp"), axis=0, tiled=True),
        lax.all_gather(key_proj, ("blk", "grp"), axis=0, tiled=True),
        lax.all_gather(value_proj, ("blk", "grp"), axis=0, tiled=True),
        lax.all_gather(attn_proj, ("blk", "grp"), axis=1, tiled=True),
        lax.all_gather(query_bias, ("blk", "grp"), axis=0, tiled=True),
        lax.all_gather(value_bias, ("blk", "grp"), axis=0, tiled=True),
        lax.all_gather(attn_bias, ("blk", "grp"), axis=0, tiled=True),
        lax.all_gather(first_gain, ("blk", "grp"), axis=0, tiled=True),
        lax.all_gather(first_shift, ("blk", "grp"), axis=0, tiled=True),
    )
    hidden_part, attn_grads, ffn_grads = block_backward(
        hidden_in, grad_total, kept_state, attn_back, ffn_back
    )
    attn_shards = (
        lax.psum_scatter(attn_grads[0], ("blk", "grp"), scatter_dimension=0, tiled=True),
        lax.psum_scatter(attn_grads[1], ("blk", "grp"), scatter_dimension=0, tiled=True),
        lax.psum_scatter(attn_grads[2], ("blk", "grp"), scatter_dimension=0, tiled=True),
        lax.psum_scatter(attn_grads[3], ("blk", "grp"), scatter_dimension=1, tiled=True),
        lax.psum_scatter(attn_grads[4], ("blk", "grp"), scatter_dimension=0, tiled=True),
        lax.psum_scatter(attn_grads[5], ("blk", "grp"), scatter_dimension=0, tiled=True),
        lax.psum_scatter(attn_grads[6], ("blk", "grp"), scatter_dimension=0, tiled=True),
        lax.psum_scatter(attn_grads[7], ("blk", "grp"), scatter_dimension=0, tiled=True),
        lax.psum_scatter(attn_grads[8], ("blk", "grp"), scatter_dimension=0, tiled=True),
    )
    ffn_shards = (
        lax.psum_scatter(ffn_grads[0], ("blk", "grp"), scatter_dimension=0, tiled=True),
        lax.psum_scatter(ffn_grads[1], ("blk", "grp"), scatter_dimension=0, tiled=True),
        lax.psum_scatter(ffn_grads[2], ("blk", "grp"), scatter_dimension=1, tiled=True),
        lax.psum_scatter(ffn_grads[3], ("blk", "grp"), scatter_dimension=0, tiled=True),
        lax.psum_scatter(ffn_grads[4], ("blk", "grp"), scatter_dimension=0, tiled=True),
        lax.psum_scatter(ffn_grads[5], ("blk", "grp"), scatter_dimension=0, tiled=True),
    )
    hidden_grad = hidden_part.astype(jnp.bfloat16).reshape(pass_count, LEN, D)
    return (
        layer_output,
        hidden_grad,
        query_acc,
        query_loss,
        attn_shards[0],
        attn_shards[1],
        attn_shards[2],
        attn_shards[3],
        attn_shards[4],
        attn_shards[5],
        attn_shards[6],
        attn_shards[7],
        attn_shards[8],
        ffn_shards[0],
        ffn_shards[1],
        ffn_shards[2],
        ffn_shards[3],
        ffn_shards[4],
        ffn_shards[5],
        cls_grad,
    )


def solution(mesh):
    in_specs = (
        P(("blk", "grp"), None, None),
        P(("blk", "grp"), None, None),
        P(("blk", "grp"), None),
        P(("blk", "grp")),
        P(("blk", "grp"), None),
        P(("blk", "grp")),
        P(("blk", "grp"), None),
        P(("blk", "grp"), None),
        P(("blk", "grp"), None),
        P(None, ("blk", "grp")),
        P(("blk", "grp")),
        P(("blk", "grp")),
        P(("blk", "grp")),
        P(("blk", "grp")),
        P(("blk", "grp")),
        P(("blk", "grp"), None),
        P(("blk", "grp")),
        P(None, ("blk", "grp")),
        P(("blk", "grp")),
        P(("blk", "grp")),
        P(("blk", "grp")),
    )
    out_specs = (
        P(("blk", "grp"), None, None),
        P(("blk", "grp"), None, None),
        P(("blk", "grp"), None),
        P(("blk", "grp")),
        P(("blk", "grp"), None),
        P(("blk", "grp"), None),
        P(("blk", "grp"), None),
        P(None, ("blk", "grp")),
        P(("blk", "grp")),
        P(("blk", "grp")),
        P(("blk", "grp")),
        P(("blk", "grp")),
        P(("blk", "grp")),
        P(("blk", "grp"), None),
        P(("blk", "grp")),
        P(None, ("blk", "grp")),
        P(("blk", "grp")),
        P(("blk", "grp")),
        P(("blk", "grp")),
        P(("blk", "grp"), None),
    )
    return jax.shard_map(local, mesh=mesh, in_specs=in_specs, out_specs=out_specs, check_vma=False)
```

profile of v0, /device:TPU:0, one launch (start us, length us, event | category | flops | bytes accessed | tf_op | source)
XLA Modules:
  0.0 1297.9 jit_solution(14908756845580786006)
XLA Ops:
  12.8 0.8 dynamic-update-slice.9
  15.3 0.8 dynamic-update-slice.3
  16.2 0.8 dynamic-update-slice.4
  18.7 0.8 dynamic-update-slice.8
  19.5 42.5 %all-reduce.20 = (bf16[768]{0:T(1024)(128)(2,1)S(1)}, bf16[768]{0:T(1024)(128)(2,1)S(1)}, bf16[768]{0:T(1024)(128)(2,1)S(1)}, bf16[768]{0:T(1024)(128)(2,1)S(1)}...) all-reduce(bf16[768]{0:T(1024)(128)(2,1)S(1)} %dynamic-update-slice, ...), channel_id=1, replica_groups=mesh['blk'=8,'grp'=4] {'blk','grp'}, use_global_device_ids=true, to_apply=%add.2 | all-reduce | flops 9216 | bytes 36864
  62.9 5.0 all-gather.8.cloned.1.call-done
  67.9 2.3 add_convert_fusion.3
  70.5 1.1 reshape.228
  71.6 52.1 %all-gather.10.cloned.1.call-done = bf16[768,768]{1,0:T(8,128)(2,1)} async-done(((bf16[24,768]{1,0:T(8,128)(2,1)}), bf16[768,768]{1,0:T(8,128)(2,1)}) %all-gather.10.cloned.1.call-update) | async-done | bytes 1179664 | tf_op jit(solution)/shard_map/all_gather | solution.py:236
  123.7 2.1 multiply_convert_fusion.2
  126.1 1.1 reshape.229
  127.1 52.5 %all-gather.12.cloned.1.call-done = bf16[768,768]{1,0:T(8,128)(2,1)} async-done(((bf16[24,768]{1,0:T(8,128)(2,1)}), bf16[768,768]{1,0:T(8,128)(2,1)}) %all-gather.12.cloned.1.call-update) | async-done | bytes 1179664 | tf_op jit(solution)/shard_map/all_gather | solution.py:237
  179.6 2.0 convolution_convert_fusion.1
  181.9 1.1 reshape.230
  183.0 2.0 fusion.87
  186.9 1.5 copy.169
  188.4 46.9 %all-gather.14.cloned.1.call-done = bf16[768,768]{0,1:T(8,128)(2,1)} async-done(((bf16[768,24]{0,1:T(8,128)(2,1)}), bf16[768,768]{0,1:T(8,128)(2,1)}) %all-gather.14.cloned.1.call-update) | async-done | bytes 1179664 | tf_op jit(solution)/shard_map/all_gather | solution.py:239
  235.3 2.6 fusion.88
  238.0 1.1 copy-done.19
  239.4 61.1 %all-gather.16.cloned.1.call-done = bf16[768,3072]{1,0:T(8,128)(2,1)} async-done(((bf16[24,3072]{1,0:T(8,128)(2,1)}), bf16[768,3072]{1,0:T(8,128)(2,1)}) %all-gather.16.cloned.1.call-update) | async-done | bytes 4718608 | tf_op jit(solution)/shard_map/all_gather | solution.py:247
  300.5 21.0 %multiply_convert_fusion = (bf16[512,3072]{1,0:T(8,128)(2,1)}, f32[512,3072]{1,0:T(8,128)}, f32[512,3072]{1,0:T(8,128)}) fusion(f32[3072]{0:T(1024)S(1)} %convert_element_type.138, bf16[768,3072]{1,0:T(8,128)(2,1)} %all-gather.16.cloned.1.call-done, f32[512,768]{1,0:T(8,128)} %copy-done.19, f32[768]{0:T(1024)S(1)} %convert_element_type.136, ...), kind=kOutput, calls=%fused_computation.4 | convolution fusion | flops 2521694208 | bytes 22042624 | tf_op jit(solution)/shard_map/dot_general | solution.py:17
  321.5 44.0 %all-gather.18.cloned.1.call-done = bf16[3072,768]{0,1:T(8,128)(2,1)} async-done(((bf16[3072,24]{0,1:T(8,128)(2,1)}), bf16[3072,768]{0,1:T(8,128)(2,1)}) %all-gather.18.cloned.1.call-update) | async-done | bytes 4718608 | tf_op jit(solution)/shard_map/all_gather | solution.py:249
  365.5 6.5 fusion.89
  373.3 0.9 copy-done.29
  374.2 69.5 %all-gather = bf16[128,1,768]{2,1,0:T(2,128)(2,1)S(1)} all-gather(bf16[4,1,768]{2,1,0:T(2,128)(2,1)S(1)} %slice.28), channel_id=2, replica_groups=mesh['blk'=8,'grp'=4] {'blk','grp'}, dimensions={0}, use_global_device_ids=true | all-gather | bytes 202752 | tf_op jit(solution)/shard_map/all_gather | solution.py:274
  445.6 1.1 fusion.78
  446.8 2.9 copy_convert_fusion
  449.7 121.9 %all-reduce.23.cloned.1.call-done = f32[128,768]{1,0:T(8,128)} async-done(((f32[128,768]{1,0:T(8,128)}), f32[128,768]{1,0:T(8,128)}) %all-reduce.23.cloned.1.call-update) | async-done | bytes 393232
  571.6 1.4 fusion.59
  573.0 2.1 fusion.84
  575.4 1.1 copy-done.3
  577.7 2.5 convert_reduce_fusion.1
  580.3 9.9 convert_reduce_fusion
  590.3 3.1 multiply_reduce_fusion.1
  594.0 1.1 copy-done.5
  595.1 2.2 fusion.32
  597.4 3.4 convolution_convert_fusion
  600.8 2.4 copy.174
  603.2 2.4 reshape.234
  605.6 2.5 convert_reduce_fusion.3
  608.8 0.9 copy-done.12
  609.7 2.2 convolution_bitcast_fusion
  611.9 3.1 copy.197
  615.3 2.5 multiply_reduce_fusion
  617.8 0.9 multiply_convert_fusion.1
  620.7 0.9 copy-done.23
  622.4 2.0 copy.193
  624.5 1.4 copy-done.9
  626.0 1.2 fusion.20
  627.8 0.9 copy-done.25
  629.5 2.0 copy.195
  631.5 1.4 copy-done.21
  632.9 7.2 fusion.80
  640.2 1.3 copy-done.18
  641.5 7.0 fusion.71
  648.5 1.0 copy-done.31
  650.4 40.5 %all-reduce.19 = (f32[768]{0:T(1024)S(1)}, f32[768]{0:T(1024)S(1)}, f32[768]{0:T(1024)S(1)}, f32[768]{0:T(1024)S(1)}, f32[768]{0:T(1024)S(1)}, /*index=5*/f32[30...) all-reduce(f32[768]{0:T(1024)S(1)} %mul.208, ...), channel_id=8, replica_groups=mesh['blk'=8,'grp'=4] {'blk','grp'}, use_global_device_ids=true, to_apply=%region_22.23.clone | all-reduce | flops 9216 | bytes 73728
  697.7 0.8 fusion.30
  699.7 1.8 add_convert_fusion.1
  701.5 97.9 %reduce-scatter.23.cloned.1.call-done = f32[24,768]{1,0:T(8,128)} async-done(((f32[768,768]{1,0:T(8,128)}), f32[24,768]{1,0:T(8,128)}) %reduce-scatter.23.cloned.1.call-update) | async-done | bytes 73744
  799.4 104.6 %reduce-scatter.19.cloned.1.call-done = f32[24,768]{1,0:T(8,128)} async-done(((f32[768,768]{1,0:T(8,128)}), f32[24,768]{1,0:T(8,128)}) %reduce-scatter.19.cloned.1.call-update) | async-done | bytes 73744
  904.1 103.9 %reduce-scatter.21.cloned.1.call-done = f32[24,768]{1,0:T(8,128)} async-done(((f32[768,768]{1,0:T(8,128)}), f32[24,768]{1,0:T(8,128)}) %reduce-scatter.21.cloned.1.call-update) | async-done | bytes 73744
  1007.9 142.1 %reduce-scatter.15.cloned.1.call-done = f32[24,3072]{1,0:T(8,128)} async-done(((f32[768,3072]{1,0:T(8,128)}), f32[24,3072]{1,0:T(8,128)}) %reduce-scatter.15.cloned.1.call-update) | async-done | bytes 294928 | tf_op jit(solution)/shard_map/reduce_scatter | solution.py:325
  1150.0 140.9 %reduce-scatter.17.cloned.1.call-done = f32[3072,24]{0,1:T(8,128)} async-done(((f32[3072,768]{0,1:T(8,128)}), f32[3072,24]{0,1:T(8,128)}) %reduce-scatter.17.cloned.1.call-update) | async-done | bytes 294928 | tf_op jit(solution)/shard_map/reduce_scatter | solution.py:327
  (166 shorter events, 32.3 us)
Async XLA Ops:
  7.2 437.3 %copy-start = (bf16[4,768]{1,0:T(4,128)(2,1)S(1)}, bf16[4,768]{1,0:T(4,128)(2,1)}, u32[]{:S(2)}) copy-start(bf16[4,768]{1,0:T(4,128)(2,1)} %param.25) | copy-start | bytes 18436
  7.2 60.7 %all-gather.8.cloned.1.call-start = ((), (), s32[]{:S(2)}) async-start(), calls=%async_computation.6 | async-start | bytes 1216512 | tf_op jit(solution)/shard_map/all_gather | solution.py:238
  7.9 115.8 %all-gather.10.cloned.1.call-start = ((), (), s32[]{:S(2)}) async-start(), calls=%async_computation.7 | async-start | bytes 1216512 | tf_op jit(solution)/shard_map/all_gather | solution.py:236
  8.7 170.9 %all-gather.12.cloned.1.call-start = ((), (), s32[]{:S(2)}) async-start(), calls=%async_computation.8 | async-start | bytes 1216512 | tf_op jit(solution)/shard_map/all_gather | solution.py:237
  9.4 225.9 %all-gather.14.cloned.1.call-start = ((), (), s32[]{:S(2)}) async-start(), calls=%async_computation.9 | async-start | bytes 1216512 | tf_op jit(solution)/shard_map/all_gather | solution.py:239
  10.0 290.5 %all-gather.16.cloned.1.call-start = ((), (), s32[]{:S(2)}) async-start(), calls=%async_computation.10 | async-start | bytes 4866048 | tf_op jit(solution)/shard_map/all_gather | solution.py:247
  10.6 354.9 %all-gather.18.cloned.1.call-start = ((), (), s32[]{:S(2)}) async-start(), calls=%async_computation.11 | async-start | bytes 4866048 | tf_op jit(solution)/shard_map/all_gather | solution.py:249
  11.2 560.5 %all-reduce.23.cloned.1.call-start = ((), (), s32[]{:S(2)}) async-start(), calls=%async_computation.18 | async-start | bytes 786432
  70.2 53.5 %copy-start.14 = (bf16[4,128,768]{2,1,0:T(8,128)(2,1)S(1)}, bf16[4,128,768]{2,1,0:T(8,128)(2,1)}, u32[]{:S(2)}) copy-start(bf16[4,128,768]{2,1,0:T(8,128)(2,1)} %param.23) | copy-start | bytes 2359300
  185.0 1.1 copy-start.27
  237.9 1.1 copy-start.19
  372.0 1.2 copy-start.2
  372.4 73.3 %copy-start.32 = (f32[4]{0:T(128)S(1)}, f32[4]{0:T(128)}, u32[]{:S(2)}) copy-start(f32[4]{0:T(128)} %param.26) | copy-start | bytes 52
  373.3 0.9 copy-start.29
  443.7 0.7 copy-start.30
  446.8 254.8 %reduce-scatter.13.cloned.1.call-start = ((), (), s32[]{:S(2)}) async-start(), calls=%async_computation.12 | async-start | bytes 2433024 | tf_op jit(solution)/shard_map/reduce_scatter | solution.py:317
  573.0 2.1 copy-start.4
  575.1 1.4 copy-start.3
  576.5 1.1 copy-start.7
  577.7 12.5 slice-start
  580.3 9.9 copy-start.17
  580.3 9.9 copy-start.20
  580.3 9.9 slice-start.1
  590.2 3.2 copy-start.35
  593.4 1.7 copy-start.22
  593.9 1.1 copy-start.5
  597.3 202.1 %reduce-scatter.23.cloned.1.call-start = ((), (), s32[]{:S(2)}) async-start(), calls=%async_computation.17 | async-start | bytes 2433024
  608.1 1.5 copy-start.15
  608.8 0.9 copy-start.12
  615.0 289.0 %reduce-scatter.19.cloned.1.call-start = ((), (), s32[]{:S(2)}) async-start(), calls=%async_computation.15 | async-start | bytes 2433024
  617.8 1.1 copy-start.11
  618.9 1.2 copy-start.8
  620.1 1.5 copy-start.16
  620.7 0.9 copy-start.23
  624.4 1.4 copy-start.9
  624.4 1.6 copy-start.10
  624.4 383.5 %reduce-scatter.21.cloned.1.call-start = ((), (), s32[]{:S(2)}) async-start(), calls=%async_computation.16 | async-start | bytes 2433024
  627.8 0.9 copy-start.25
  631.4 1.4 copy-start.21
  631.5 518.5 %reduce-scatter.15.cloned.1.call-start = ((), (), s32[]{:S(2)}) async-start(), calls=%async_computation.13 | async-start | bytes 9732096 | tf_op jit(solution)/shard_map/reduce_scatter | solution.py:325
  640.1 1.4 copy-start.18
  640.1 650.7 %reduce-scatter.17.cloned.1.call-start = ((), (), s32[]{:S(2)}) async-start(), calls=%async_computation.14 | async-start | bytes 9732096 | tf_op jit(solution)/shard_map/reduce_scatter | solution.py:327
  648.5 1.0 copy-start.31
  648.5 47.7 %copy-start.26 = (bf16[4,128,12,64]{1,0,3,2:T(4,128)(2,1)S(1)}, bf16[4,128,12,64]{1,0,3,2:T(4,128)(2,1)}, u32[]{:S(2)}) copy-start(bf16[4,128,12,64]{1,0,3,2:T(4,128)(2,1)} %copy-done.25) | copy-start | bytes 2359300
  648.5 47.7 %copy-start.34 = (bf16[768,768]{1,0:T(8,128)(2,1)S(1)}, bf16[768,768]{1,0:T(8,128)(2,1)}, u32[]{:S(2)}) copy-start(bf16[768,768]{1,0:T(8,128)(2,1)} %all-gather.12.cloned.1.call-done) | copy-start | bytes 3538948
  696.2 1.1 copy-start.24
  696.2 1.5 copy-start.33
  697.7 1.4 copy-start.6
  697.7 1.6 copy-start.13
  697.7 2.0 copy-start.28
  699.7 591.2 %copy-start.1 = (bf16[4,768]{1,0:T(4,128)(2,1)S(1)}, bf16[4,768]{1,0:T(4,128)(2,1)}, u32[]{:S(2)}) copy-start(bf16[4,768]{1,0:T(4,128)(2,1)} %param.25) | copy-start | bytes 18436
Sparse Core Ops, SparseCore 0:
  10.8 56.9 all-gather.7
  70.7 52.9 all-gather.9
  126.5 53.0 all-gather.11
  182.2 53.0 all-gather.13
  238.0 62.4 all-gather.15
  303.1 62.3 all-gather.17
  446.9 124.6 all-reduce.22
  597.5 98.0 reduce-scatter.12
  701.5 97.9 reduce-scatter.22
  806.0 98.0 reduce-scatter.18
  909.9 97.9 reduce-scatter.20
  1015.3 134.6 reduce-scatter.14
  1156.5 134.3 reduce-scatter.16
where the time goes:
time: 1310 us; the launch traced here: 1300 us
  waiting for transfers between devices  977 us (75%)
  blocking collectives  153 us (12%)
  matrix products  88.3 us (7%)
  local copies, waits for them, and re-layouts  50.3 us (4%)
  between operations  15 us (1%)
  other arithmetic  14.3 us (1%)
    unnamed x17, waiting for transfers between devices  432 us
    reduce_scatter x1, waiting for transfers between devices, local(): lax.psum_scatter(ffn_grads[0], ('blk', 'grp'), scatter_dimension=0, tiled...  142 us
    reduce_scatter x1, waiting for transfers between devices, local(): lax.psum_scatter(ffn_grads[2], ('blk', 'grp'), scatter_dimension=1, tiled...  141 us
    unnamed x2, blocking collectives  83 us
    dot_general x19, matrix products, product(): return jnp.dot(left_side, right_side, preferred_element_type=jnp.float32)  77.5 us
    all_gather x1, blocking collectives, local(): cls_piece = lax.all_gather(cls_local, ('blk', 'grp'), axis=0, tiled=True)  69.5 us
    all_gather x1, waiting for transfers between devices, local(): lax.all_gather(inner_proj, ('blk', 'grp'), axis=0, tiled=True)  61.1 us
    all_gather x1, waiting for transfers between devices, local(): lax.all_gather(key_proj, ('blk', 'grp'), axis=0, tiled=True)  52.5 us
  transfers between devices with their start and end apart: 13, of which 12 were waited for; matrix products, arithmetic and copies ran while one was open for 8% of the time, Pallas kernels for 0%

commit v1 on v0

--- a/solution.py
+++ b/solution.py
@@ -1,6 +1,8 @@
 import jax
 import jax.numpy as jnp
 from jax import lax
+from jax.experimental import pallas as pl
+from jax.experimental.pallas import tpu as pltpu
 from jax.sharding import PartitionSpec as P
 
 D = 768
@@ -209,7 +211,7 @@
     return (hidden_grad, attn_grads, ffn_grads)
 
 
-def local(
+def plain_local(
     hidden_in,
     upstream_grad,
     query_vectors,
@@ -354,6 +356,970 @@
     )
 
 
+BF = jnp.bfloat16
+F32 = jnp.float32
+MESH = pl.DeviceIdType.MESH
+VM = pl.BlockSpec(memory_space=pltpu.VMEM)
+DMA = pltpu.SemaphoreType.DMA
+ALL = slice(None)
+VMEM_LIMIT = 60 * 2**20
+NC = 12
+LW = 384
+ROWS = 24
+TOK = 512
+
+
+class Place:
+    def __init__(self):
+        self.b = lax.axis_index("blk")
+        self.z = lax.axis_index("grp")
+        self.y, self.x, self.c = self.b // 4, (self.b // 2) % 2, self.b % 2
+        self.zh, self.zl = self.z // 2, self.z % 2
+        self.mid = ((self.z + 1) // 2) % 2
+        self.xdev = (self.b + 2 - 4 * self.x, self.z)
+        self.ydev = (self.b + 4 - 8 * self.y, self.z)
+        self.cdev = (self.b + 1 - 2 * self.c, self.z)
+        self.zdev = (self.b, self.z + 1 - 2 * self.zl)
+        self.fdev = (self.b, 3 - self.z)
+
+
+def greet(p):
+    bar = pltpu.get_barrier_semaphore()
+    for k in range(1, 8):
+        pl.semaphore_signal(bar, 1, device_id=((p.b + k) % 8, p.z), device_id_type=MESH)
+    for k in range(1, 4):
+        pl.semaphore_signal(bar, 1, device_id=(p.b, (p.z + k) % 4), device_id_type=MESH)
+    pl.semaphore_wait(bar, 10)
+
+
+def rcopy(src, dst, ss, rs, dev):
+    return pltpu.make_async_remote_copy(
+        src_ref=src, dst_ref=dst, send_sem=ss, recv_sem=rs, device_id=dev, device_id_type=MESH
+    )
+
+
+class Flow:
+    def __init__(self, p, ref, kind, ss, rs):
+        self.p, self.ref, self.kind, self.ss, self.rs = p, ref, kind, ss, rs
+        self.f, self.s = (p.x, p.y) if kind == 0 else (p.y, p.x)
+        self.fdev, self.sdev = (p.xdev, p.ydev) if kind == 0 else (p.ydev, p.xdev)
+
+    def at(self, f, s, zz, c=None):
+        c = self.p.c if c is None else c
+        return self.ref.at[self.index(f, s, zz, c)]
+
+    def index(self, f, s, zz, c):
+        return (s, f, c, zz) if self.kind == 0 else (f, s, c, zz)
+
+    def copy(self, stage, src, dst, dev):
+        return rcopy(src, dst, self.ss(stage), self.rs(stage), dev)
+
+    def go(self, stage, view, dev):
+        self.copy(stage, view, view, dev).start()
+
+    def got(self, stage, view):
+        self.copy(stage, view, view, self.p.cdev).wait_recv()
+
+    def sent(self, stage, view):
+        self.copy(stage, view, view, self.p.cdev).wait_send()
+
+
+class Gather(Flow):
+    def s2_send(self):
+        self.go(0, self.at(self.f, self.s, self.p.zh), self.fdev)
+
+    def s2_recv(self):
+        self.got(0, self.at(1 - self.f, self.s, self.p.zh))
+
+    def s3a_send(self):
+        self.go(1, self.at(ALL, self.s, self.p.zh), self.p.fdev)
+
+    def s3a_recv(self):
+        self.got(1, self.at(ALL, self.s, 1 - self.p.zh))
+
+    def s3b_send(self):
+        self.go(2, self.at(ALL, self.s, 1 - self.p.zh), self.p.zdev)
+
+    def s3b_recv(self):
+        self.got(2, self.at(ALL, self.s, 1 - self.p.zh))
+
+    def s4_send(self):
+        self.go(3, self.at(ALL, self.s, ALL), self.sdev)
+
+    def s4_recv(self):
+        self.got(3, self.at(ALL, 1 - self.s, ALL))
+
+    def c1_send(self):
+        self.go(4, self.at(ALL, self.s, ALL), self.p.cdev)
+
+    def c1_recv(self):
+        self.got(4, self.at(ALL, self.s, ALL, 1 - self.p.c))
+
+    def c2_send(self):
+        self.go(5, self.at(ALL, 1 - self.s, ALL), self.p.cdev)
+
+    def c2_recv(self):
+        self.got(5, self.at(ALL, 1 - self.s, ALL, 1 - self.p.c))
+
+    def drain(self):
+        self.sent(0, self.at(self.f, self.s, self.p.zh))
+
+        @pl.when(self.p.mid == 1)
+        def _():
+            self.sent(1, self.at(ALL, self.s, self.p.zh))
+            self.sent(2, self.at(ALL, self.s, 1 - self.p.zh))
+
+        self.sent(3, self.at(ALL, self.s, ALL))
+        self.sent(4, self.at(ALL, self.s, ALL))
+        self.sent(5, self.at(ALL, 1 - self.s, ALL))
+
+
+def lanes_of(ci):
+    return pl.ds(pl.multiple_of((ci % 2) * LW, 128), LW)
+
+
+class Scatter(Flow):
+    def __init__(self, p, ref, kind, ss, rs, bufs):
+        super().__init__(p, ref, kind, ss, rs)
+        self.rc, self.r4, self.r3b, self.r3a, self.r2 = bufs
+
+    def add(self, stage, buf, f, s, zz):
+        self.copy(stage, buf, buf, self.p.cdev).wait_recv()
+        at = self.index(f, s, zz, self.p.c)
+        self.ref[at] = (self.ref[at].astype(F32) + buf[...].astype(F32)).astype(BF)
+
+    def t0_send(self):
+        self.copy(0, self.at(ALL, ALL, ALL, 1 - self.p.c), self.rc, self.p.cdev).start()
+
+    def t0_add(self):
+        self.add(0, self.rc, ALL, ALL, ALL)
+
+    def t1_send(self):
+        self.copy(1, self.at(ALL, 1 - self.s, ALL), self.r4, self.sdev).start()
+
+    def t1_add(self):
+        self.add(1, self.r4, ALL, self.s, ALL)
+
+    def t2a_send(self):
+        self.copy(2, self.at(ALL, self.s, 1 - self.p.zh), self.r3b, self.p.zdev).start()
+
+    def t2a_add(self):
+        self.add(2, self.r3b, ALL, self.s, 1 - self.p.zh)
+
+    def t2b_send(self):
+        self.copy(3, self.at(ALL, self.s, 1 - self.p.zh), self.r3a, self.p.fdev).start()
+
+    def t2b_add(self):
+        self.add(3, self.r3a, ALL, self.s, self.p.zh)
+
+    def t3_send(self):
+        self.copy(4, self.at(1 - self.f, self.s, self.p.zh), self.r2, self.fdev).start()
+
+    def t3_sum(self):
+        self.copy(4, self.r2, self.r2, self.p.cdev).wait_recv()
+        at = self.index(self.f, self.s, self.p.zh, self.p.c)
+        return self.ref[at].astype(F32) + self.r2[...].astype(F32)
+
+    def drain(self):
+        self.sent(0, self.at(ALL, ALL, ALL, 1 - self.p.c))
+        self.sent(1, self.at(ALL, 1 - self.s, ALL))
+
+        @pl.when(self.p.mid == 0)
+        def _():
+            self.sent(2, self.at(ALL, self.s, 1 - self.p.zh))
+
+        @pl.when(self.p.mid == 1)
+        def _():
+            self.sent(3, self.at(ALL, self.s, 1 - self.p.zh))
+
+        self.sent(4, self.at(1 - self.f, self.s, self.p.zh))
+
+
+def nn(a, b): return lax.dot_general(a, b, (((1,), (0,)), ((), ())), preferred_element_type=F32)
+def nt(a, b): return lax.dot_general(a, b, (((1,), (1,)), ((), ())), preferred_element_type=F32)
+def tn(a, b): return lax.dot_general(a, b, (((0,), (0,)), ((), ())), preferred_element_type=F32)
+
+def weight(ref, i): return ref[i].reshape(D, D)
+def keep(ref, i, val): ref[i] = val.astype(BF).reshape(2, 2, 2, 2, 48, D)
+
+def tiles(n, body, unroll=None):
+    def f(r, c):
+        body(pl.ds(pl.multiple_of(r * (TOK // n), TOK // n), TOK // n)); return c
+    lax.fori_loop(0, n, f, 0, unroll=unroll)
+
+def masks():
+    lane = lax.broadcasted_iota(jnp.int32, (1, 128), 1)
+    lo = (lane < 64).astype(F32).astype(BF)
+    return lo, (1 - lo.astype(F32)).astype(BF)
+
+def qkv(s, MT=2):
+    def body(r):
+        x = s.x[r, :]
+        s.q[r, :] = ((nn(x, weight(s.wa, 1)) + s.vec[0:1, :]) * 0.125).astype(BF)
+        s.k[r, :] = nn(x, weight(s.wb, 1)).astype(BF)
+        s.v[r, :] = (nn(x, weight(s.wa, 0)) + s.vec[1:2, :]).astype(BF)
+    tiles(MT, body)
+
+def split(x, lo, hi): return jnp.concatenate([x * lo, x * hi], 0)
+
+def attn_fwd(s, p):
+    lo, hi = masks()
+    r = pl.ds(pl.multiple_of(p * 128, 128), 128)
+    for h in range(6):
+        ln = pl.ds(h * 128, 128)
+        sc = nt(s.q[r, ln], split(s.k[r, ln], lo, hi))
+        out = []
+        for w in (sc[:, :128], sc[:, 128:]):
+            e = jnp.exp(w - jnp.max(w, axis=1, keepdims=True))
+            out.append((e * (1.0 / jnp.sum(e, axis=1, keepdims=True))).astype(BF))
+        pr = jnp.concatenate(out, 1)
+        s.p[p, h] = pr
+        s.ctx[r, ln] = nn(pr, split(s.v[r, ln], lo, hi)).astype(BF)
+
+def normalize(res):
+    c = res - jnp.mean(res, axis=1, keepdims=True)
+    inv = lax.rsqrt(jnp.mean(c * c, axis=1, keepdims=True) + NORM_EPS)
+    return c * inv, inv
+
+def attn_out(s, n=8):
+    def body(r):
+        s.acc[r, :] = nt(s.ctx[r, :], weight(s.wb, 0))
+    tiles(2, body)
+    def body(r):
+        n_, inv = normalize(s.x[r, :].astype(F32) + s.acc[r, :] + s.vec[2:3, :])
+        s.fn[r, :] = n_
+        s.s1[r, :] = inv
+        s.nl[r, :] = (n_ * s.vec[3:4, :] + s.vec[4:5, :]).astype(BF)
+        s.acc[r, :] = n_ * s.vec[3:4, :] + s.vec[4:5, :] + s.vec[5:6, :]
+    tiles(n * 2, body)
+
+def gelu_parts(x):
+    ax = jnp.abs(x) * 0.7071067811865476
+    t = 1.0 / (1.0 + 0.3275911 * ax)
+    e = jnp.exp(x * x * -0.5)
+    poly = t * (0.254829592 + t * (-0.284496736 + t * (1.421413741 + t * (-1.453152027 + t * 1.061405429))))
+    half = 0.5 * poly * e
+    phi = jnp.where(x > 0, 1.0 - half, half)
+    return phi, e * 0.3989422804014327
+
+def ffn_fwd(s, j, gelu=True):
+    def body(r):
+        s.tmp[r, :] = nn(s.nl[r, :], weight(s.wa, 2 + j))
+    tiles(2, body)
+    def ew(r):
+        x = s.tmp[r, :] + s.vec[pl.ds(8 + j, 1), :]
+        cdf, pdf = gelu_parts(x)
+        s.act[j, r, :] = (x * cdf).astype(BF)
+        s.gp[j, r, :] = (cdf + x * pdf).astype(BF)
+    tiles(32, ew)
+    def body(r):
+        s.acc[r, :] += nt(s.act[j, r, :], weight(s.wb, 2 + j))
+    tiles(2, body)
+
+def norm2(s):
+    def body(r):
+        n_, inv = normalize(s.acc[r, :])
+        s.acc[r, :] = n_
+        s.s2[r, :] = inv
+        s.lo[r, :] = (n_ * s.vec[6:7, :] + s.vec[7:8, :]).astype(BF)
+    tiles(16, body)
+
+def norm_back(g, n_, inv, gain):
+    sg = g * gain
+    return inv * (sg - jnp.mean(sg, axis=1, keepdims=True) - n_ * jnp.mean(sg * n_, axis=1, keepdims=True))
+
+def colsum(x): return jnp.sum(x.reshape(-1, 8, x.shape[-1]), axis=0)
+
+def norm2_back(s):
+    s.gv[...] = jnp.zeros_like(s.gv)
+    def body(r):
+        g = s.up[r, :].astype(F32)
+        n_ = s.acc[r, :]
+        s.gv[6] += colsum(g * n_)
+        s.gv[7] += colsum(g)
+        res = norm_back(g, n_, s.s2[r, :], s.vec[6:7, :])
+        s.acc[r, :] = res
+        b = res.astype(BF)
+        s.bg[r, :] = b
+        s.gv[5] += colsum(b.astype(F32))
+    tiles(16, body)
+
+def ffn_back(s, j):
+    def body(r):
+        s.tmp[r, :] = nn(s.bg[r, :], weight(s.wb, 2 + j))
+    tiles(2, body)
+    keep(s.wb, 2 + j, tn(s.bg[...], s.act[j]))
+    def ew(r):
+        ig = (s.tmp[r, :] * s.gp[j, r, :].astype(F32)).astype(BF)
+        s.gp[j, r, :] = ig
+        s.gv[8 + j] += colsum(ig.astype(F32))
+    tiles(16, ew)
+    def body(r):
+        s.acc[r, :] += nt(s.gp[j, r, :], weight(s.wa, 2 + j))
+    tiles(2, body)
+    keep(s.wa, 2 + j, tn(s.nl[...], s.gp[j]))
+
+def norm1_back(s):
+    def body(r):
+        g = s.acc[r, :]
+        n_ = s.fn[r, :]
+        s.gv[3] += colsum(g * n_)
+        s.gv[4] += colsum(g)
+        res = norm_back(g, n_, s.s1[r, :], s.vec[3:4, :])
+        s.acc[r, :] = res
+        b = res.astype(BF)
+        s.bg[r, :] = b
+        s.gv[2] += colsum(b.astype(F32))
+    tiles(16, body)
+    def body(r):
+        s.nl[r, :] = nn(s.bg[r, :], weight(s.wb, 0)).astype(BF)
+    tiles(2, body)
+    keep(s.wb, 0, tn(s.bg[...], s.ctx[...]))
+
+def attn_back(s, p):
+    lo, hi = masks()
+    r = pl.ds(pl.multiple_of(p * 128, 128), 128)
+    for h in range(6):
+        ln = pl.ds(h * 128, 128)
+        qp, kp, vp, cg = s.q[r, ln], s.k[r, ln], s.v[r, ln], s.nl[r, ln]
+        dp = nt(cg, split(vp, lo, hi))
+        pr = s.p[p, h]
+        prf = pr.astype(F32)
+        t = prf * dp
+        ds = []
+        for a, b in ((0, 128), (128, 256)):
+            ds.append((t[:, a:b] - prf[:, a:b] * jnp.sum(t[:, a:b], axis=1, keepdims=True)).astype(BF))
+        dq = nn(jnp.concatenate(ds, 1), split(kp, lo, hi))
+        dk = tn(jnp.concatenate(ds, 0), split(qp, lo, hi))
+        dv = tn(jnp.concatenate([pr[:, :128], pr[:, 128:]], 0), split(cg, lo, hi))
+        s.q[r, ln] = dq.astype(BF)
+        s.k[r, ln] = dk.astype(BF)
+        s.v[r, ln] = dv.astype(BF)
+
+def qkv_back(s):
+    def body(r):
+        h = s.acc[r, :] + 0.125 * nt(s.q[r, :], weight(s.wa, 1))
+        h += nt(s.k[r, :], weight(s.wb, 1))
+        h += nt(s.v[r, :], weight(s.wa, 0))
+        s.hg[r, :] = h.astype(BF)
+    tiles(2, body)
+    def sums(r):
+        s.gv[0] += colsum(s.q[r, :].astype(F32)) * 0.125
+        s.gv[1] += colsum(s.v[r, :].astype(F32))
+    tiles(8, sums)
+    keep(s.wa, 0, tn(s.x[...], s.v[...]))
+    keep(s.wa, 1, tn(s.x[...], s.q[...]) * 0.125)
+    keep(s.wb, 1, tn(s.x[...], s.k[...]))
+
+
+class Bag:
+    pass
+
+
+def column_maps(width, offset, first):
+    lane = lax.broadcasted_iota(jnp.int32, (128, D), 0).astype(F32)
+    col = lax.broadcasted_iota(jnp.int32, (128, D), 1).astype(F32) + first
+    owner = jnp.floor((col + 0.5) * (1.0 / width))
+    hot = ((lane - offset) == (col - owner * width)).astype(F32)
+    return hot, owner[0:1]
+
+
+def unpack_small(s):
+    sm = s.small[...].reshape(32, 32, 128)[:, :8].reshape(256, 128)
+    hot, owner = column_maps(24, 0, 0.0)
+    dev = jnp.floor((lax.broadcasted_iota(jnp.int32, (256, 1), 0).astype(F32) + 0.5) * 0.125)
+    wide = jnp.where(dev == owner, nn(sm.astype(BF), hot.astype(BF)), 0.0)
+    s.vec[0:8, :] = jnp.sum(wide.reshape(32, 8, D), axis=0)
+    one = s.small[pl.ds(0, 32, stride=32), :].astype(BF)
+    dev32 = lax.broadcasted_iota(jnp.int32, (32, 1), 0).astype(F32)
+    rows = []
+    for j in range(4):
+        hot, owner = column_maps(96, 24, float(D * j))
+        part = jnp.where(dev32 == owner, nn(one, hot.astype(BF)), 0.0)
+        rows.append(jnp.sum(part, axis=0, keepdims=True))
+    s.vec[8:16, :] = jnp.concatenate(rows + [jnp.zeros((4, D), F32)], 0)
+    hot, owner = column_maps(4, 120, 0.0)
+    part = lax.dot_general(
+        sm, hot[:, :128], (((1,), (0,)), ((), ())), precision=lax.Precision.HIGHEST, preferred_element_type=F32
+    )
+    part = jnp.where(dev == owner[:, :128], part, 0.0)
+    s.aux[...] = jnp.sum(part.reshape(32, 8, 128), axis=0)
+    for q in range(4):
+        for k in range(6):
+            piece = s.small[pl.ds(8 + 6 * q + k, 32, stride=32), :]
+            s.qm[pl.ds(k * 128 + q, 32, stride=4), :] = piece
+
+
+def all_queries(s):
+    return jnp.concatenate([s.qm[k * 128 : (k + 1) * 128, :] for k in range(6)], 1).astype(BF)
+
+
+def first_rows(s):
+    rows = [s.acc[p * LEN : p * LEN + 8, :][0:1] for p in range(4)]
+    n_, inv = normalize(jnp.concatenate(rows + [jnp.zeros((4, D), F32)], 0))
+    s.cn[...] = n_
+    s.ci[...] = inv
+    cls = (n_ * s.vec[6:7, :] + s.vec[7:8, :]).astype(BF)
+    s.cls[...] = cls.astype(F32)
+    return nt(cls, all_queries(s))
+
+
+def loss_part(s, me):
+    scores = s.sc[...]
+    row = lax.broadcasted_iota(jnp.int32, (256, 1), 0).astype(F32)
+    dev = jnp.floor((row + 0.5) * 0.125)
+    slot = row - 8.0 * dev
+    real = slot < 4.0
+    passage = 4.0 * dev + slot
+    ids, count, weight_q = s.aux[0:3, :], s.aux[3:4, :], s.aux[4:5, :]
+
+    def hits(passage):
+        return (
+            (ids[0:1] == passage)
+            | ((ids[1:2] == passage) & (count > 1.5))
+            | ((ids[2:3] == passage) & (count > 2.5))
+        )
+
+    everyone = jnp.where(real, scores, NEG_FILL)
+    masked = jnp.where(hits(passage) & real, scores, NEG_FILL)
+    totals = []
+    for part in (everyone, masked):
+        top = jnp.max(part, axis=0, keepdims=True)
+        totals.append(top + jnp.log(jnp.sum(jnp.exp(part - top), axis=0, keepdims=True)))
+    total_all, total_pos = totals
+    s.loss[...] = jnp.broadcast_to(total_all - total_pos, (8, 128))
+    own = s.sc[pl.ds(pl.multiple_of(me * 8, 8), 8), :]
+    slot = lax.broadcasted_iota(jnp.int32, (8, 128), 0)
+    hit = hits((4 * me + slot).astype(F32))
+    pull = jnp.where(hit, jnp.exp(own - total_pos), 0.0)
+    grad = weight_q * (jnp.exp(own - total_all) - pull)
+    grad = jnp.where(slot < 4, grad, 0.0).astype(BF)
+    s.cgrad[...] = nn(grad, all_queries(s))
+    part = tn(grad, s.cls[...].astype(BF))
+    for k in range(6):
+        s.qpart[k * 128 : (k + 1) * 128, :] = part[:, k * 128 : (k + 1) * 128]
+
+
+def query_rows(s):
+    for q in range(4):
+        for k in range(6):
+            piece = s.qpart[pl.ds(k * 128 + q, 32, stride=4), :]
+            s.qrow[pl.ds(6 * q + k, 32, stride=24), :] = piece
+    s.qg[...] = s.qrow[...].astype(BF).reshape(2, 2, 2, 2, 48, 128)
+
+
+def add_cls(s):
+    g = jnp.concatenate([s.up[p * LEN : p * LEN + 16, :][0:1].astype(F32) for p in range(4)] + [jnp.zeros((4, D), F32)], 0)
+    extra = s.cgrad[...]
+    live = (lax.broadcasted_iota(jnp.int32, (8, 1), 0) < 4).astype(F32)
+    n_, inv = s.cn[...] * live, s.ci[...]
+    s.gv[6] += extra * n_
+    s.gv[7] += extra
+    res = norm_back(g + extra, n_, inv, s.vec[6:7, :]) * live
+    old = norm_back(g, n_, inv, s.vec[6:7, :]) * live
+    low = res.astype(BF).astype(F32)
+    s.gv[5] += low - old.astype(BF).astype(F32)
+    top = (lax.broadcasted_iota(jnp.int32, (16, 1), 0) == 0)
+    for p in range(4):
+        at = slice(p * LEN, p * LEN + 16)
+        s.acc[at, :] = jnp.where(top, res[p : p + 1], s.acc[at, :])
+        s.bg[at, :] = jnp.where(top, low[p : p + 1], s.bg[at, :].astype(F32)).astype(BF)
+
+
+OUTS = dict(
+    lo=((TOK, D), BF),
+    hg=((TOK, D), BF),
+    out=((6, 48, D), F32),
+    q_out=((ROWS, 128), F32),
+    bias_out=((16, D), F32),
+    loss=((8, 128), F32),
+    cgrad=((8, D), F32),
+)
+INS = ("x", "up", "pack", "tile")
+SCRATCH = dict(
+    wa=((6, 2, 2, 2, 2, 48, D), BF),
+    wb=((6, 2, 2, 2, 2, 48, D), BF),
+    rb=((6, 48, D), BF),
+    q=((TOK, D), BF),
+    k=((TOK, D), BF),
+    v=((TOK, D), BF),
+    ctx=((TOK, D), BF),
+    p=((4, 6, 128, 256), BF),
+    fn=((TOK, D), F32),
+    s1=((TOK, 1), F32),
+    s2=((TOK, 1), F32),
+    nl=((TOK, D), BF),
+    acc=((TOK, D), F32),
+    act=((4, TOK, D), BF),
+    gp=((4, TOK, D), BF),
+    bg=((TOK, D), BF),
+    tmp=((TOK, D), F32),
+    small=((1024, 128), F32),
+    sc=((256, 128), F32),
+    vec=((16, D), F32),
+    gv=((12, 8, D), F32),
+    aux=((8, 128), F32),
+    qm=((D, 128), F32),
+    cn=((8, D), F32),
+    ci=((8, 1), F32),
+    cls=((8, D), F32),
+    qpart=((D, 128), F32),
+    qrow=((D, 128), F32),
+    qg=((2, 2, 2, 2, 48, 128), BF),
+    rc=((2, NC, 2, 2, 2, 48, LW), BF),
+    r4=((2, NC, 2, 2, 48, LW), BF),
+    r3b=((2, NC, 2, 48, LW), BF),
+    r3a=((2, NC, 2, 48, LW), BF),
+    r2=((2, NC, 48, LW), BF),
+    st=((NC, 48, LW), BF),
+    r1=((NC, 48, LW), BF),
+    qc=((2, 2, 2, 48, 128), BF),
+    q4=((2, 2, 48, 128), BF),
+    q3b=((2, 48, 128), BF),
+    q3a=((2, 48, 128), BF),
+    q2=((48, 128), BF),
+    qst=((32, 128), BF),
+    q1=((32, 128), BF),
+    bs_buf=((5, 16, D), F32),
+    br_buf=((5, 16, D), F32),
+)
+SEMS = dict(
+    gs=(6, 2, NC),
+    gr=(6, 2, NC),
+    g1s=(NC,),
+    g1r=(NC,),
+    ss=(5, 2, NC),
+    rs=(5, 2, NC),
+    s1s=(NC,),
+    s1r=(NC,),
+    qss=(6,),
+    qrs=(6,),
+    bss=(5,),
+    brs=(5,),
+    zs=(2, 4),
+    zr=(2, 4),
+    bs=(2, 8),
+    br=(2, 8),
+)
+
+
+class Spread:
+    def __init__(self, p, s, ref, which, rows):
+        self.p, self.s, self.ref, self.which, self.rows = p, s, ref, which, rows
+
+    def zview(self, z):
+        r = self.rows
+        return self.ref.at[pl.ds(pl.multiple_of((self.p.b * 4 + z) * r, r), r), :]
+
+    def bview(self, b):
+        r = self.rows * 4
+        return self.ref.at[pl.ds(pl.multiple_of(b * r, r), r), :]
+
+    def zcopy(self, k, view):
+        p, s, w = self.p, self.s, self.which
+        return rcopy(view, view, s.zs.at[w, k], s.zr.at[w, k], (p.b, (p.z + k) % 4))
+
+    def bcopy(self, k, view):
+        p, s, w = self.p, self.s, self.which
+        return rcopy(view, view, s.bs.at[w, k], s.br.at[w, k], ((p.b + k) % 8, p.z))
+
+    def first(self):
+        for k in range(1, 4):
+            self.zcopy(k, self.zview(self.p.z)).start()
+
+    def second(self):
+        for k in range(1, 4):
+            self.zcopy(k, self.zview((self.p.z + 4 - k) % 4)).wait_recv()
+        for k in range(1, 8):
+            self.bcopy(k, self.bview(self.p.b)).start()
+
+    def finish(self):
+        for k in range(1, 8):
+            self.bcopy(k, self.bview((self.p.b + 8 - k) % 8)).wait_recv()
+        for k in range(1, 4):
+            self.zcopy(k, self.zview(self.p.z)).wait_send()
+        for k in range(1, 8):
+            self.bcopy(k, self.bview(self.p.b)).wait_send()
+
+
+def gather_steps(p, s):
+    def flows(ci):
+        out = []
+        for kind, ref in ((0, s.wa), (1, s.wb)):
+            view = ref.at[ci // 2, :, :, :, :, :, lanes_of(ci)]
+            out.append(
+                Gather(
+                    p,
+                    view,
+                    kind,
+                    lambda st, kind=kind: s.gs.at[st, kind, ci],
+                    lambda st, kind=kind: s.gr.at[st, kind, ci],
+                )
+            )
+        return out
+
+    def s1(ci):
+        at = (ci // 2, ALL, lanes_of(ci))
+        return rcopy(s.pack.at[at], s.rb.at[at], s.g1s.at[ci], s.g1r.at[ci], p.zdev)
+
+    def merge(ci):
+        s1(ci).wait_recv()
+        i, ln = ci // 2, lanes_of(ci)
+        own = s.pack[i, :, ln].astype(F32)
+        oth = s.rb[i, :, ln].astype(F32)
+        first = p.zl == 0
+        lo = jnp.where(first, own, oth)
+        hi = jnp.where(first, oth, own)
+        s.wa[i, p.y, p.x, p.c, p.zh, :, ln] = jnp.concatenate([lo[:ROWS], hi[:ROWS]], 0).astype(BF)
+        s.wb[i, p.y, p.x, p.c, p.zh, :, ln] = jnp.concatenate([lo[ROWS:], hi[ROWS:]], 0).astype(BF)
+        for f in flows(ci):
+            f.s2_send()
+
+    def s23(ci):
+        for f in flows(ci):
+            f.s2_recv()
+
+        @pl.when(p.mid == 1)
+        def _():
+            for f in flows(ci):
+                f.s3a_send()
+
+    def s34(ci):
+        @pl.when(p.mid == 1)
+        def _():
+            for f in flows(ci):
+                f.s3a_recv()
+            for f in flows(ci):
+                f.s3b_send()
+
+        @pl.when(p.mid == 0)
+        def _():
+            for f in flows(ci):
+                f.s3b_recv()
+
+        for f in flows(ci):
+            f.s4_send()
+        for f in flows(ci):
+            f.c1_send()
+
+    def s45(ci):
+        for f in flows(ci):
+            f.s4_recv()
+            f.c2_send()
+
+    def core(ci):
+        for f in flows(ci):
+            f.c1_recv()
+            f.c2_recv()
+            f.drain()
+        s1(ci).wait_send()
+
+    @pl.loop(0, NC)
+    def _(ci):
+        s1(ci).start()
+
+    return ((0, merge), (2, s23), (4, s34), (5, s45), (6, core))
+
+
+def scatter_steps(p, s):
+    def piece(ci):
+        return (ci // 2 + 2) % 6
+
+    def flows(ci):
+        made = []
+        for kind, ref in ((0, s.wa), (1, s.wb)):
+            bufs = tuple(buf.at[kind, ci] for buf in (s.rc, s.r4, s.r3b, s.r3a, s.r2))
+            made.append(
+                Scatter(
+                    p,
+                    ref.at[piece(ci), :, :, :, :, :, lanes_of(ci)],
+                    kind,
+                    lambda st, kind=kind: s.ss.at[st, kind, ci],
+                    lambda st, kind=kind: s.rs.at[st, kind, ci],
+                    bufs,
+                )
+            )
+        return made
+
+    def k0(fs):
+        for f in fs:
+            f.t0_send()
+
+    def k1(fs):
+        for f in fs:
+            f.t0_add()
+            f.t1_send()
+
+    def k2(fs):
+        for f in fs:
+            f.t1_add()
+
+        @pl.when(p.mid == 0)
+        def _():
+            for f in fs:
+                f.t2a_send()
+
+    def k3(fs):
+        @pl.when(p.mid == 1)
+        def _():
+            for f in fs:
+                f.t2a_add()
+                f.t2b_send()
+
+    def k4(fs):
+        @pl.when(p.mid == 1)
+        def _():
+            for f in fs:
+                f.t2b_add()
+
+        for f in fs:
+            f.t3_send()
+
+    first = p.zl == 0
+
+    def halves(total):
+        top, low = total[:ROWS], total[ROWS:]
+        return jnp.where(first, top, low), jnp.where(first, low, top)
+
+    def s1(ci):
+        return rcopy(s.st.at[ci], s.r1.at[ci], s.s1s.at[ci], s.s1r.at[ci], p.zdev)
+
+    def k5(ci):
+        fa, fb = flows(ci)
+        keep_a, give_a = halves(fa.t3_sum())
+        keep_b, give_b = halves(fb.t3_sum())
+        s.st[ci] = jnp.concatenate([give_a, give_b], 0).astype(BF)
+        s1(ci).start()
+        s.out[piece(ci), :, lanes_of(ci)] = jnp.concatenate([keep_a, keep_b], 0)
+
+    def k6(ci):
+        s1(ci).wait_recv()
+        at = (piece(ci), ALL, lanes_of(ci))
+        s.out[at] = s.out[at] + s.r1[ci].astype(F32)
+        for f in flows(ci):
+            f.drain()
+        s1(ci).wait_send()
+
+    stages = (
+        (0, lambda ci: k0(flows(ci))),
+        (1, lambda ci: k1(flows(ci))),
+        (2, lambda ci: k2(flows(ci))),
+        (4, lambda ci: k3(flows(ci))),
+        (6, lambda ci: k4(flows(ci))),
+        (8, k5),
+        (9, k6),
+    )
+    q = Scatter(
+        p, s.qg, 0, lambda st: s.qss.at[st], lambda st: s.qrs.at[st], (s.qc, s.q4, s.q3b, s.q3a, s.q2)
+    )
+    q1 = rcopy(s.qst, s.q1, s.qss.at[5], s.qrs.at[5], p.zdev)
+
+    def q5():
+        keep, give = halves(q.t3_sum())
+        s.qst[...] = jnp.concatenate([give, jnp.zeros((8, 128), F32)], 0).astype(BF)
+        q1.start()
+        s.q_out[...] = keep
+
+    def q6():
+        q1.wait()
+        s.q_out[...] = s.q_out[...] + s.q1[:ROWS].astype(F32)
+        q.drain()
+
+    query_steps = [lambda fn=fn: fn([q]) for fn in (k0, k1, k2, k3, k4)] + [q5, q6]
+    devs = (p.cdev, p.xdev, p.ydev, p.zdev, (p.b, (p.z + 2) % 4))
+
+    def bcopy(k):
+        return rcopy(s.bs_buf.at[k], s.br_buf.at[k], s.bss.at[k], s.brs.at[k], devs[k])
+
+    def bias_step(k):
+        if k == 0:
+            total = jnp.concatenate([jnp.sum(s.gv[...], axis=1), jnp.zeros((4, D), F32)], 0)
+        else:
+            bcopy(k - 1).wait()
+            total = s.bs_buf[k - 1] + s.br_buf[k - 1]
+        if k < 5:
+            s.bs_buf[k] = total
+            bcopy(k).start()
+        else:
+            s.bias_out[...] = total
+
+    return stages, query_steps, [lambda k=k: bias_step(k) for k in range(6)]
+
+
+def run_stages(stages, t):
+    for off, fn in stages:
+
+        @pl.when((t >= off) & (t < NC + off))
+        def _(off=off, fn=fn):
+            fn(t - off)
+
+
+def run_at(t, table):
+    for when, fn in table:
+
+        @pl.when(t == when)
+        def _(fn=fn):
+            fn()
+
+
+def layer_kernel(*refs):
+    s = Bag()
+    names = list(INS) + list(OUTS) + list(SCRATCH) + list(SEMS)
+    for name, ref in zip(names, refs):
+        setattr(s, name, ref)
+    p = Place()
+    greet(p)
+    me = p.b * 4 + p.z
+    vectors = Spread(p, s, s.small, 0, 32)
+    scores = Spread(p, s, s.sc, 1, 8)
+    s.small[pl.ds(pl.multiple_of(me * 32, 32), 32), :] = s.tile[...]
+    vectors.first()
+    stages = gather_steps(p, s)
+
+    def passages(fn, lo):
+        def go():
+            pl.loop(lo, lo + 2)(lambda i: fn(s, i))
+
+        return go
+
+    def small_done():
+        vectors.finish()
+        unpack_small(s)
+
+    forward = (
+        (3, vectors.second),
+        (7, small_done),
+        (9, lambda: qkv(s)),
+        (10, passages(attn_fwd, 0)),
+        (11, passages(attn_fwd, 2)),
+        (12, lambda: attn_out(s)),
+    )
+
+    @pl.loop(0, NC + 6)
+    def _(t):
+        run_stages(stages, t)
+        run_at(t, forward)
+
+        @pl.when((t >= 13) & (t <= 15))
+        def _():
+            ffn_fwd(s, t - 13)
+
+        @pl.when(t == 17)
+        def _():
+            ffn_fwd(s, 3)
+
+    s.sc[pl.ds(pl.multiple_of(me * 8, 8), 8), :] = first_rows(s)
+    scores.first()
+    s.gv[...] = jnp.zeros_like(s.gv)
+    norm2(s)
+    scores.second()
+    norm2_back(s)
+    scores.finish()
+    loss_part(s, me)
+    add_cls(s)
+
+    stages, query_steps, bias_steps = scatter_steps(p, s)
+    ffn_back(s, 0)
+    backward = [
+        (3, lambda: norm1_back(s)),
+        (4, passages(attn_back, 0)),
+        (5, passages(attn_back, 2)),
+        (6, lambda: qkv_back(s)),
+        (7, lambda: query_rows(s)),
+    ]
+    backward += [(8 + k, fn) for k, fn in enumerate(query_steps)]
+    backward += [(9 + 2 * k, fn) for k, fn in enumerate(bias_steps)]
+
+    @pl.loop(0, NC + 9)
+    def _(t):
+        run_stages(stages, t)
+
+        @pl.when(t < 3)
+        def _():
+            ffn_back(s, t + 1)
+
+        run_at(t, backward)
+
+
+def layer(x, up, pack, tile):
+    return pl.pallas_call(
+        layer_kernel,
+        out_shape=tuple(jax.ShapeDtypeStruct(*o) for o in OUTS.values()),
+        in_specs=[VM] * 4,
+        out_specs=(VM,) * len(OUTS),
+        scratch_shapes=[pltpu.VMEM(*b) for b in SCRATCH.values()] + [DMA(n) for n in SEMS.values()],
+        compiler_params=pltpu.CompilerParams(
+            collective_id=1, has_side_effects=True, vmem_limit_bytes=VMEM_LIMIT
+        ),
+    )(x, up, pack, tile)
+
+
+def fast_local(
+    hidden_in,
+    upstream_grad,
+    query_vectors,
+    loss_weight,
+    positive_ids,
+    positive_count,
+    query_proj,
+    key_proj,
+    value_proj,
+    attn_proj,
+    query_bias,
+    value_bias,
+    attn_bias,
+    first_gain,
+    first_shift,
+    inner_proj,
+    inner_bias,
+    outer_proj,
+    outer_bias,
+    second_gain,
+    second_shift,
+):
+    outer_t = outer_proj.T
+    pairs = [(value_proj, attn_proj.T), (query_proj, key_proj)]
+    pairs += [(inner_proj[:, j * D : (j + 1) * D], outer_t[:, j * D : (j + 1) * D]) for j in range(4)]
+    pack = jnp.stack([jnp.concatenate(pair, 0) for pair in pairs])
+    vecs = jnp.stack(
+        [query_bias, value_bias, attn_bias, first_gain, first_shift, outer_bias, second_gain, second_shift]
+    ).astype(F32)
+    mid = jnp.zeros((8, 96), F32).at[0].set(inner_bias.astype(F32))
+    aux = jnp.concatenate(
+        [positive_ids.T.astype(F32), positive_count[None].astype(F32), loss_weight[None], jnp.zeros((3, 4), F32)], 0
+    )
+    tile = jnp.concatenate([vecs, mid, aux, jnp.zeros((8, 4), F32)], 1)
+    tile = jnp.concatenate([tile, query_vectors.astype(F32).reshape(ROWS, 128)], 0)
+    layer_output, hidden_grad, out, query_acc, bias, loss, cls_grad = layer(
+        hidden_in.reshape(TOK, D), upstream_grad.reshape(TOK, D), pack, tile
+    )
+    me = lax.axis_index("blk") * 4 + lax.axis_index("grp")
+    vec = lax.dynamic_slice(bias[:8], (0, ROWS * me), (8, ROWS))
+    inner_vec = lax.dynamic_slice(bias[8:12].reshape(-1), (96 * me,), (96,))
+    return (
+        layer_output.reshape(hidden_in.shape),
+        hidden_grad.reshape(hidden_in.shape),
+        query_acc.reshape(4, D),
+        lax.dynamic_slice(loss[0], (4 * me,), (4,)),
+        out[1, :ROWS],
+        out[1, ROWS:],
+        out[0, :ROWS],
+        out[0, ROWS:].T,
+        vec[0],
+        vec[1],
+        vec[2],
+        vec[3],
+        vec[4],
+        jnp.concatenate([out[j, :ROWS] for j in range(2, 6)], 1),
+        inner_vec,
+        jnp.concatenate([out[j, ROWS:] for j in range(2, 6)], 1).T,
+        vec[5],
+        vec[6],
+        vec[7],
+        cls_grad[:4],
+    )
+
+
 def solution(mesh):
     in_specs = (
         P(("blk", "grp"), None, None),
@@ -400,4 +1366,6 @@
         P(("blk", "grp")),
         P(("blk", "grp"), None),
     )
+    tiled = mesh.shape["blk"] == 8 and mesh.shape["grp"] == 4
+    local = fast_local if tiled else plain_local
     return jax.shard_map(local, mesh=mesh, in_specs=in_specs, out_specs=out_specs, check_vma=False)

time: 1310 us -> 198 us (0.15)
  waiting for transfers between devices: 977 us -> 0 us
  Pallas kernels: 0 us -> 179 us
  blocking collectives: 153 us -> 0 us
  matrix products: 88.3 us -> 0 us
  local copies, waits for them, and re-layouts: 50.3 us -> 14.1 us
  between operations: 15 us -> 0.79 us
    unnamed x17 -> x0, waiting for transfers between devices: 432 us -> none
    reduce_scatter x3 -> x0, waiting for transfers between devices: 283 us -> none  [the longest x1 142 us: local(): lax.psum_scatter(ffn_grads[0], ('blk', 'grp'), scatter_dimension=0, tiled...]
    all_gather x6 -> x0, waiting for transfers between devices: 262 us -> none  [the longest x1 61.1 us: local(): lax.all_gather(inner_proj, ('blk', 'grp'), axis=0, tiled=True)]
    pallas_call x0 -> x1, Pallas kernels: none -> 179 us  [layer(): pl.pallas_call(layer_kernel, out_shape=tuple((jax.ShapeDtypeStruct(*o) fo...]
    dot_general x27 -> x0, matrix products: 88.3 us -> none  [the longest x19 77.5 us: product(): return jnp.dot(left_side, right_side, preferred_element_type=jnp.float32)]
    unnamed x2 -> x0, blocking collectives: 83 us -> none
    all_gather x1 -> x0, blocking collectives: 69.5 us -> none  [local(): cls_piece = lax.all_gather(cls_local, ('blk', 'grp'), axis=0, tiled=True)]
    unnamed x108 -> x21, local copies, waits for them, and re-layouts: 37.6 us -> 4.6 us
  transfers between devices with their start and end apart: 13 -> 0, of which waited for: 12 -> 0; matrix products, arithmetic and copies ran while one was open for 8% -> 0% of each run, Pallas kernels for 0% -> 0%
where the time goes in v1:
time: 198 us
  Pallas kernels  179 us (90%)
  local copies, waits for them, and re-layouts  14.1 us (7%)
  other arithmetic  4.21 us (2%)
    pallas_call x1, Pallas kernels, layer(): pl.pallas_call(layer_kernel, out_shape=tuple((jax.ShapeDtypeStruct(*o) fo...  179 us
    unnamed x21, local copies, waits for them, and re-layouts  4.6 us

profile of v1, /device:TPU:0, one launch (start us, length us, event | category | flops | bytes accessed | tf_op | source)
XLA Modules:
  0.0 197.8 jit_solution(395772959784693948)
XLA Ops:
  0.7 0.0 copy-start.3
  0.7 0.7 convert_bitcast_fusion.1
  1.4 0.8 copy.41
  2.1 0.8 stack.63
  2.9 0.7 pad_convert_fusion
  3.6 0.7 reshape.105
  4.3 1.3 pad_maximum_fusion.1.refs_3_
  5.6 0.0 copy-done.3
  5.6 0.0 copy-start.4
  5.6 0.0 copy-start.5
  5.6 0.9 fusion.6
  6.5 0.0 copy-done.4
  6.5 0.0 copy-done.5
  6.5 0.0 copy-start.6
  6.5 0.0 copy-start.7
  6.6 0.7 copy-done.6
  7.3 0.0 copy-done.7
  7.4 0.0 copy-start.2
  7.4 0.8 copy-done.2
  8.1 178.7 %shard_map.356 = (bf16[512,768]{1,0:T(8,128)(2,1)}, bf16[512,768]{1,0:T(8,128)(2,1)}, f32[6,48,768]{2,1,0:T(8,128)}, f32[24,128]{1,0:T(8,128)}, f32[16,768]{1,0:...) custom-call(bf16[512,768]{1,0:T(8,128)(2,1)} %bitcast.92, bf16[512,768]{1,0:T(8,128)(2,1)} %bitcast.93, ...), custom_call_target="tpu_custom_call" | custom-call | tf_op jit(solution)/shard_map/pallas_call | solution.py:1245
  186.9 0.0 copy-start.8
  186.9 0.7 slice.118
  187.6 0.6 dynamic-slice_bitcast_fusion
  188.2 1.3 reshape.102
  189.5 1.3 slice.141
  190.8 0.0 copy-done.8
  190.8 0.1 constant_dynamic-slice_fusion
  190.9 0.6 dynamic_slice.14
  191.5 0.5 slice_bitcast_fusion.12
  192.0 2.0 %slice_bitcast_fusion.3 = (f32[24,768]{1,0:T(8,128)S(1)}, f32[24,768]{1,0:T(8,128)S(1)}, f32[24,768]{1,0:T(8,128)S(1)}, f32[24,768]{1,0:T(8,128)S(1)}, f32[24,76...) fusion(f32[6,48,768]{2,1,0:T(8,128)} %get-tuple-element.43), kind=kLoop, calls=%fused_computation.17 | loop fusion | bytes 1769472 | tf_op jit(solution)/shard_map/squeeze | solution.py:1315
  194.0 0.0 copy-start.1
  194.0 0.7 maximum_bitcast_fusion
  194.8 0.7 pad_maximum_fusion
  195.5 0.0 copy-done.1
  195.5 0.0 copy-start
  195.5 0.9 copy.49
  196.4 0.5 copy-done
  196.9 0.9 copy.50
  (13 shorter events, 0.1 us)
Async XLA Ops:
  0.7 5.0 %copy-start.3 = (bf16[24,3072]{1,0:T(8,128)(2,1)S(1)}, bf16[24,3072]{1,0:T(8,128)(2,1)}, u32[]{:S(2)}) copy-start(bf16[24,3072]{1,0:T(8,128)(2,1)} %param.38) | copy-start | bytes 442372
  5.6 0.9 copy-start.4
  5.6 0.9 copy-start.5
  6.5 0.8 copy-start.6
  6.5 0.8 copy-start.7
  7.4 0.8 copy-start.2
  186.9 3.9 %copy-start.8 = (f32[16,768]{1,0:T(8,128)S(1)}, f32[16,768]{1,0:T(8,128)}, u32[]{:S(2)}) copy-start(f32[16,768]{1,0:T(8,128)} %get-tuple-element.44) | copy-start | bytes 147460
  194.0 1.5 copy-start.1
  195.5 1.4 copy-start

commit v2 on v1

--- a/solution.py
+++ b/solution.py
@@ -363,8 +363,9 @@
 DMA = pltpu.SemaphoreType.DMA
 ALL = slice(None)
 VMEM_LIMIT = 60 * 2**20
-NC = 12
 LW = 384
+PARTS = 2
+NC = 6 * PARTS
 ROWS = 24
 TOK = 512
 
@@ -399,14 +400,14 @@
 
 
 class Flow:
-    def __init__(self, p, ref, kind, ss, rs):
-        self.p, self.ref, self.kind, self.ss, self.rs = p, ref, kind, ss, rs
+    def __init__(self, p, ref, kind, ss, rs, lead=()):
+        self.p, self.ref, self.kind, self.ss, self.rs, self.lead = p, ref, kind, ss, rs, lead
         self.f, self.s = (p.x, p.y) if kind == 0 else (p.y, p.x)
         self.fdev, self.sdev = (p.xdev, p.ydev) if kind == 0 else (p.ydev, p.xdev)
 
     def at(self, f, s, zz, c=None):
         c = self.p.c if c is None else c
-        return self.ref.at[self.index(f, s, zz, c)]
+        return self.ref.at[self.lead + self.index(f, s, zz, c)]
 
     def index(self, f, s, zz, c):
         return (s, f, c, zz) if self.kind == 0 else (f, s, c, zz)
@@ -443,11 +444,15 @@
     def s3b_recv(self):
         self.got(2, self.at(ALL, self.s, 1 - self.p.zh))
 
-    def s4_send(self):
-        self.go(3, self.at(ALL, self.s, ALL), self.sdev)
+    def s4a_send(self):
+        self.go(3, self.at(ALL, self.s, self.p.zh), self.sdev)
+
+    def s4b_send(self):
+        self.go(6, self.at(ALL, self.s, 1 - self.p.zh), self.sdev)
 
     def s4_recv(self):
-        self.got(3, self.at(ALL, 1 - self.s, ALL))
+        self.got(3, self.at(ALL, 1 - self.s, self.p.zh))
+        self.got(6, self.at(ALL, 1 - self.s, 1 - self.p.zh))
 
     def c1_send(self):
         self.go(4, self.at(ALL, self.s, ALL), self.p.cdev)
@@ -469,19 +474,20 @@
             self.sent(1, self.at(ALL, self.s, self.p.zh))
             self.sent(2, self.at(ALL, self.s, 1 - self.p.zh))
 
-        self.sent(3, self.at(ALL, self.s, ALL))
+        self.sent(3, self.at(ALL, self.s, self.p.zh))
+        self.sent(6, self.at(ALL, self.s, 1 - self.p.zh))
         self.sent(4, self.at(ALL, self.s, ALL))
         self.sent(5, self.at(ALL, 1 - self.s, ALL))
 
 
 def lanes_of(ci):
-    return pl.ds(pl.multiple_of((ci % 2) * LW, 128), LW)
+    return pl.ds(pl.multiple_of((ci % PARTS) * LW, 128), LW)
 
 
 class Scatter(Flow):
-    def __init__(self, p, ref, kind, ss, rs, bufs):
-        super().__init__(p, ref, kind, ss, rs)
-        self.rc, self.r4, self.r3b, self.r3a, self.r2 = bufs
+    def __init__(self, p, ref, kind, ss, rs, bufs, lead=()):
+        super().__init__(p, ref, kind, ss, rs, lead)
+        self.rc, self.r4a, self.r4b, self.r3b, self.r3a, self.r2 = bufs
 
     def add(self, stage, buf, f, s, zz):
         self.copy(stage, buf, buf, self.p.cdev).wait_recv()
@@ -494,11 +500,17 @@
     def t0_add(self):
         self.add(0, self.rc, ALL, ALL, ALL)
 
-    def t1_send(self):
-        self.copy(1, self.at(ALL, 1 - self.s, ALL), self.r4, self.sdev).start()
-
-    def t1_add(self):
-        self.add(1, self.r4, ALL, self.s, ALL)
+    def t1a_send(self):
+        self.copy(1, self.at(ALL, 1 - self.s, 1 - self.p.zh), self.r4a, self.sdev).start()
+
+    def t1a_add(self):
+        self.add(1, self.r4a, ALL, self.s, 1 - self.p.zh)
+
+    def t1b_send(self):
+        self.copy(5, self.at(ALL, 1 - self.s, self.p.zh), self.r4b, self.sdev).start()
+
+    def t1b_add(self):
+        self.add(5, self.r4b, ALL, self.s, self.p.zh)
 
     def t2a_send(self):
         self.copy(2, self.at(ALL, self.s, 1 - self.p.zh), self.r3b, self.p.zdev).start()
@@ -522,7 +534,8 @@
 
     def drain(self):
         self.sent(0, self.at(ALL, ALL, ALL, 1 - self.p.c))
-        self.sent(1, self.at(ALL, 1 - self.s, ALL))
+        self.sent(1, self.at(ALL, 1 - self.s, 1 - self.p.zh))
+        self.sent(5, self.at(ALL, 1 - self.s, self.p.zh))
 
         @pl.when(self.p.mid == 0)
         def _():
@@ -552,13 +565,11 @@
     lo = (lane < 64).astype(F32).astype(BF)
     return lo, (1 - lo.astype(F32)).astype(BF)
 
-def qkv(s, MT=2):
-    def body(r):
-        x = s.x[r, :]
-        s.q[r, :] = ((nn(x, weight(s.wa, 1)) + s.vec[0:1, :]) * 0.125).astype(BF)
-        s.k[r, :] = nn(x, weight(s.wb, 1)).astype(BF)
-        s.v[r, :] = (nn(x, weight(s.wa, 0)) + s.vec[1:2, :]).astype(BF)
-    tiles(MT, body)
+def qkv(s):
+    x = s.x[...]
+    s.q[...] = ((nn(x, weight(s.wa, 0)) + s.vec[0:1, :]) * 0.125).astype(BF)
+    s.k[...] = nn(x, weight(s.wb, 0)).astype(BF)
+    s.v[...] = (nn(x, weight(s.wa, 1)) + s.vec[1:2, :]).astype(BF)
 
 def split(x, lo, hi): return jnp.concatenate([x * lo, x * hi], 0)
 
@@ -582,16 +593,14 @@
     return c * inv, inv
 
 def attn_out(s, n=8):
-    def body(r):
-        s.acc[r, :] = nt(s.ctx[r, :], weight(s.wb, 0))
-    tiles(2, body)
+    s.acc[...] = nt(s.ctx[...], weight(s.wb, 1))
     def body(r):
         n_, inv = normalize(s.x[r, :].astype(F32) + s.acc[r, :] + s.vec[2:3, :])
         s.fn[r, :] = n_
         s.s1[r, :] = inv
         s.nl[r, :] = (n_ * s.vec[3:4, :] + s.vec[4:5, :]).astype(BF)
         s.acc[r, :] = n_ * s.vec[3:4, :] + s.vec[4:5, :] + s.vec[5:6, :]
-    tiles(n * 2, body)
+    tiles(2, body)
 
 def gelu_parts(x):
     ax = jnp.abs(x) * 0.7071067811865476
@@ -602,19 +611,17 @@
     phi = jnp.where(x > 0, 1.0 - half, half)
     return phi, e * 0.3989422804014327
 
-def ffn_fwd(s, j, gelu=True):
-    def body(r):
-        s.tmp[r, :] = nn(s.nl[r, :], weight(s.wa, 2 + j))
-    tiles(2, body)
-    def ew(r):
-        x = s.tmp[r, :] + s.vec[pl.ds(8 + j, 1), :]
+def ffn_fwd(s, h):
+    j, ln = h // PARTS, lanes_of(h)
+    w_in = s.wa[2 + j, :, :, :, :, :, ln].reshape(D, LW)
+    w_out = s.wb[2 + j, :, :, :, :, :, ln].reshape(D, LW)
+    for r in (slice(0, 256), slice(256, 512)):
+        x = nn(s.nl[r, :], w_in) + s.vec[pl.ds(8 + j, 1), ln]
         cdf, pdf = gelu_parts(x)
-        s.act[j, r, :] = (x * cdf).astype(BF)
-        s.gp[j, r, :] = (cdf + x * pdf).astype(BF)
-    tiles(32, ew)
-    def body(r):
-        s.acc[r, :] += nt(s.act[j, r, :], weight(s.wb, 2 + j))
-    tiles(2, body)
+        act = (x * cdf).astype(BF)
+        s.act[j, r, ln] = act
+        s.gp[j, r, ln] = (cdf + x * pdf).astype(BF)
+        s.acc[r, :] += nt(act, w_out)
 
 def norm2(s):
     def body(r):
@@ -622,7 +629,7 @@
         s.acc[r, :] = n_
         s.s2[r, :] = inv
         s.lo[r, :] = (n_ * s.vec[6:7, :] + s.vec[7:8, :]).astype(BF)
-    tiles(16, body)
+    tiles(2, body)
 
 def norm_back(g, n_, inv, gain):
     sg = g * gain
@@ -631,7 +638,6 @@
 def colsum(x): return jnp.sum(x.reshape(-1, 8, x.shape[-1]), axis=0)
 
 def norm2_back(s):
-    s.gv[...] = jnp.zeros_like(s.gv)
     def body(r):
         g = s.up[r, :].astype(F32)
         n_ = s.acc[r, :]
@@ -642,21 +648,17 @@
         b = res.astype(BF)
         s.bg[r, :] = b
         s.gv[5] += colsum(b.astype(F32))
-    tiles(16, body)
+    tiles(2, body)
 
 def ffn_back(s, j):
-    def body(r):
-        s.tmp[r, :] = nn(s.bg[r, :], weight(s.wb, 2 + j))
-    tiles(2, body)
+    s.tmp[...] = nn(s.bg[...], weight(s.wb, 2 + j))
     keep(s.wb, 2 + j, tn(s.bg[...], s.act[j]))
     def ew(r):
         ig = (s.tmp[r, :] * s.gp[j, r, :].astype(F32)).astype(BF)
         s.gp[j, r, :] = ig
         s.gv[8 + j] += colsum(ig.astype(F32))
-    tiles(16, ew)
-    def body(r):
-        s.acc[r, :] += nt(s.gp[j, r, :], weight(s.wa, 2 + j))
-    tiles(2, body)
+    tiles(2, ew)
+    s.acc[...] += nt(s.gp[j], weight(s.wa, 2 + j))
     keep(s.wa, 2 + j, tn(s.nl[...], s.gp[j]))
 
 def norm1_back(s):
@@ -670,11 +672,9 @@
         b = res.astype(BF)
         s.bg[r, :] = b
         s.gv[2] += colsum(b.astype(F32))
-    tiles(16, body)
-    def body(r):
-        s.nl[r, :] = nn(s.bg[r, :], weight(s.wb, 0)).astype(BF)
     tiles(2, body)
-    keep(s.wb, 0, tn(s.bg[...], s.ctx[...]))
+    s.nl[...] = nn(s.bg[...], weight(s.wb, 1)).astype(BF)
+    keep(s.wb, 1, tn(s.bg[...], s.ctx[...]))
 
 def attn_back(s, p):
     lo, hi = masks()
@@ -697,19 +697,16 @@
         s.v[r, ln] = dv.astype(BF)
 
 def qkv_back(s):
-    def body(r):
-        h = s.acc[r, :] + 0.125 * nt(s.q[r, :], weight(s.wa, 1))
-        h += nt(s.k[r, :], weight(s.wb, 1))
-        h += nt(s.v[r, :], weight(s.wa, 0))
-        s.hg[r, :] = h.astype(BF)
-    tiles(2, body)
+    s.acc[...] += 0.125 * nt(s.q[...], weight(s.wa, 0))
+    s.acc[...] += nt(s.k[...], weight(s.wb, 0))
+    s.hg[...] = (s.acc[...] + nt(s.v[...], weight(s.wa, 1))).astype(BF)
     def sums(r):
         s.gv[0] += colsum(s.q[r, :].astype(F32)) * 0.125
         s.gv[1] += colsum(s.v[r, :].astype(F32))
-    tiles(8, sums)
-    keep(s.wa, 0, tn(s.x[...], s.v[...]))
-    keep(s.wa, 1, tn(s.x[...], s.q[...]) * 0.125)
-    keep(s.wb, 1, tn(s.x[...], s.k[...]))
+    tiles(2, sums)
+    keep(s.wa, 1, tn(s.x[...], s.v[...]))
+    keep(s.wa, 0, tn(s.x[...], s.q[...]) * 0.125)
+    keep(s.wb, 0, tn(s.x[...], s.k[...]))
 
 
 class Bag:
@@ -725,12 +722,12 @@
 
 
 def unpack_small(s):
-    sm = s.small[...].reshape(32, 32, 128)[:, :8].reshape(256, 128)
+    sm = s.small[...]
     hot, owner = column_maps(24, 0, 0.0)
     dev = jnp.floor((lax.broadcasted_iota(jnp.int32, (256, 1), 0).astype(F32) + 0.5) * 0.125)
     wide = jnp.where(dev == owner, nn(sm.astype(BF), hot.astype(BF)), 0.0)
     s.vec[0:8, :] = jnp.sum(wide.reshape(32, 8, D), axis=0)
-    one = s.small[pl.ds(0, 32, stride=32), :].astype(BF)
+    one = s.small[pl.ds(0, 32, stride=8), :].astype(BF)
     dev32 = lax.broadcasted_iota(jnp.int32, (32, 1), 0).astype(F32)
     rows = []
     for j in range(4):
@@ -744,9 +741,13 @@
     )
     part = jnp.where(dev == owner[:, :128], part, 0.0)
     s.aux[...] = jnp.sum(part.reshape(32, 8, 128), axis=0)
+
+
+def unpack_queries(s):
+    s.qrow[...] = s.qx[...].reshape(D, 128).astype(F32)
     for q in range(4):
         for k in range(6):
-            piece = s.small[pl.ds(8 + 6 * q + k, 32, stride=32), :]
+            piece = s.qrow[pl.ds(6 * q + k, 32, stride=24), :]
             s.qm[pl.ds(k * 128 + q, 32, stride=4), :] = piece
 
 
@@ -826,20 +827,29 @@
         s.bg[at, :] = jnp.where(top, low[p : p + 1], s.bg[at, :].astype(F32)).astype(BF)
 
 
+HBM = pl.BlockSpec(memory_space=pl.ANY)
+MERGES, G_S23, G_S4A, G_S34, G_S45, G_END = 2, 1, 2, 3, 5, 6
+S_K1, S_K1B, S_K2, S_K3, S_K4, S_K5, S_K6 = 1, 3, 2, 3, 10, 11, 12
+S_FAST = 2
+S_END = S_K6 + NC // S_FAST
 OUTS = dict(
-    lo=((TOK, D), BF),
-    hg=((TOK, D), BF),
+    lo_out=((TOK, D), BF),
+    hg_out=((TOK, D), BF),
     out=((6, 48, D), F32),
     q_out=((ROWS, 128), F32),
     bias_out=((16, D), F32),
     loss=((8, 128), F32),
     cgrad=((8, D), F32),
 )
-INS = ("x", "up", "pack", "tile")
+INS = ("x_in", "up_in", "pack", "tile", "qpack")
 SCRATCH = dict(
     wa=((6, 2, 2, 2, 2, 48, D), BF),
     wb=((6, 2, 2, 2, 2, 48, D), BF),
     rb=((6, 48, D), BF),
+    x=((TOK, D), BF),
+    up=((TOK, D), BF),
+    lo=((TOK, D), BF),
+    hg=((TOK, D), BF),
     q=((TOK, D), BF),
     k=((TOK, D), BF),
     v=((TOK, D), BF),
@@ -854,7 +864,9 @@
     gp=((4, TOK, D), BF),
     bg=((TOK, D), BF),
     tmp=((TOK, D), F32),
-    small=((1024, 128), F32),
+    small=((256, 128), F32),
+    qx=((2, 2, 2, 2, 48, 128), BF),
+    qrb=((32, 128), BF),
     sc=((256, 128), F32),
     vec=((16, D), F32),
     gv=((12, 8, D), F32),
@@ -867,14 +879,16 @@
     qrow=((D, 128), F32),
     qg=((2, 2, 2, 2, 48, 128), BF),
     rc=((2, NC, 2, 2, 2, 48, LW), BF),
-    r4=((2, NC, 2, 2, 48, LW), BF),
+    r4a=((2, NC, 2, 48, LW), BF),
+    r4b=((2, NC, 2, 48, LW), BF),
     r3b=((2, NC, 2, 48, LW), BF),
     r3a=((2, NC, 2, 48, LW), BF),
     r2=((2, NC, 48, LW), BF),
     st=((NC, 48, LW), BF),
     r1=((NC, 48, LW), BF),
     qc=((2, 2, 2, 48, 128), BF),
-    q4=((2, 2, 48, 128), BF),
+    q4a=((2, 48, 128), BF),
+    q4b=((2, 48, 128), BF),
     q3b=((2, 48, 128), BF),
     q3a=((2, 48, 128), BF),
     q2=((48, 128), BF),
@@ -884,22 +898,19 @@
     br_buf=((5, 16, D), F32),
 )
 SEMS = dict(
-    gs=(6, 2, NC),
-    gr=(6, 2, NC),
-    g1s=(NC,),
+    gs=(7, 2),
+    gr=(7, 2, NC),
+    g1s=(1,),
     g1r=(NC,),
-    ss=(5, 2, NC),
-    rs=(5, 2, NC),
-    s1s=(NC,),
-    s1r=(NC,),
-    qss=(6,),
-    qrs=(6,),
+    xs=(8,),
+    xr=(8,),
     bss=(5,),
     brs=(5,),
     zs=(2, 4),
     zr=(2, 4),
     bs=(2, 8),
     br=(2, 8),
+    io=(4,),
 )
 
 
@@ -946,96 +957,131 @@
     def flows(ci):
         out = []
         for kind, ref in ((0, s.wa), (1, s.wb)):
-            view = ref.at[ci // 2, :, :, :, :, :, lanes_of(ci)]
+            view = ref.at[ci // PARTS, :, :, :, :, :, lanes_of(ci)]
             out.append(
                 Gather(
                     p,
                     view,
                     kind,
-                    lambda st, kind=kind: s.gs.at[st, kind, ci],
+                    lambda st, kind=kind: s.gs.at[st, kind],
                     lambda st, kind=kind: s.gr.at[st, kind, ci],
                 )
             )
         return out
 
     def s1(ci):
-        at = (ci // 2, ALL, lanes_of(ci))
-        return rcopy(s.pack.at[at], s.rb.at[at], s.g1s.at[ci], s.g1r.at[ci], p.zdev)
+        at = (ci // PARTS, ALL, lanes_of(ci))
+        return rcopy(s.pack.at[at], s.rb.at[at], s.g1s.at[0], s.g1r.at[ci], p.zdev)
+
+    first = p.zl == 0
+
+    def order(own, oth):
+        return jnp.where(first, own, oth), jnp.where(first, oth, own)
 
     def merge(ci):
         s1(ci).wait_recv()
-        i, ln = ci // 2, lanes_of(ci)
-        own = s.pack[i, :, ln].astype(F32)
-        oth = s.rb[i, :, ln].astype(F32)
-        first = p.zl == 0
-        lo = jnp.where(first, own, oth)
-        hi = jnp.where(first, oth, own)
+        i, ln = ci // PARTS, lanes_of(ci)
+        lo, hi = order(s.pack[i, :, ln].astype(F32), s.rb[i, :, ln].astype(F32))
         s.wa[i, p.y, p.x, p.c, p.zh, :, ln] = jnp.concatenate([lo[:ROWS], hi[:ROWS]], 0).astype(BF)
         s.wb[i, p.y, p.x, p.c, p.zh, :, ln] = jnp.concatenate([lo[ROWS:], hi[ROWS:]], 0).astype(BF)
         for f in flows(ci):
             f.s2_send()
 
-    def s23(ci):
-        for f in flows(ci):
+    def s23(fs):
+        for f in fs:
             f.s2_recv()
 
         @pl.when(p.mid == 1)
         def _():
-            for f in flows(ci):
+            for f in fs:
                 f.s3a_send()
 
-    def s34(ci):
+    def s4a(fs):
+        for f in fs:
+            f.s4a_send()
+
+    def s34(fs):
         @pl.when(p.mid == 1)
         def _():
-            for f in flows(ci):
+            for f in fs:
                 f.s3a_recv()
-            for f in flows(ci):
                 f.s3b_send()
 
         @pl.when(p.mid == 0)
         def _():
-            for f in flows(ci):
+            for f in fs:
                 f.s3b_recv()
 
-        for f in flows(ci):
-            f.s4_send()
-        for f in flows(ci):
+        for f in fs:
+            f.s4b_send()
             f.c1_send()
 
-    def s45(ci):
-        for f in flows(ci):
+    def s45(fs):
+        for f in fs:
             f.s4_recv()
             f.c2_send()
 
-    def core(ci):
-        for f in flows(ci):
+    def core(fs):
+        for f in fs:
             f.c1_recv()
             f.c2_recv()
-            f.drain()
-        s1(ci).wait_send()
+
+    def drain():
+        for kind, ref in ((0, s.wa), (1, s.wb)):
+            sems = lambda st, kind=kind: s.gs.at[st, kind]
+            Gather(p, ref, kind, sems, sems, (ALL,)).drain()
+        rcopy(s.pack, s.rb, s.g1s.at[0], s.g1r.at[0], p.zdev).wait_send()
+        q.drain()
 
     @pl.loop(0, NC)
     def _(ci):
         s1(ci).start()
 
-    return ((0, merge), (2, s23), (4, s34), (5, s45), (6, core))
+    q = Gather(p, s.qx, 0, lambda st: s.xs.at[st], lambda st: s.xr.at[st])
+    q1 = rcopy(s.qpack, s.qrb, s.xs.at[7], s.xr.at[7], p.zdev)
+    q1.start()
+
+    def qmerge():
+        q1.wait()
+        lo, hi = order(s.qpack[...].astype(F32), s.qrb[...].astype(F32))
+        s.qx[p.y, p.x, p.c, p.zh] = jnp.concatenate([lo[:ROWS], hi[:ROWS]], 0).astype(BF)
+        q.s2_send()
+
+    def q23():
+        s23([q])
+        s4a([q])
+
+    query_steps = [qmerge, q23, lambda: s34([q]), lambda: s45([q]), lambda: core([q])]
+
+    def pack_of(fn):
+        return lambda ci: fn(flows(ci))
+
+    stages = (
+        (0, MERGES, merge),
+        (G_S23, 1, pack_of(s23)),
+        (G_S4A, 1, pack_of(s4a)),
+        (G_S34, 1, pack_of(s34)),
+        (G_S45, 1, pack_of(s45)),
+        (G_END, 1, pack_of(core)),
+    )
+    return stages, query_steps, drain
 
 
 def scatter_steps(p, s):
     def piece(ci):
-        return (ci // 2 + 2) % 6
+        return (ci // PARTS + 2) % 6
 
     def flows(ci):
         made = []
         for kind, ref in ((0, s.wa), (1, s.wb)):
-            bufs = tuple(buf.at[kind, ci] for buf in (s.rc, s.r4, s.r3b, s.r3a, s.r2))
+            bufs = tuple(buf.at[kind, ci] for buf in (s.rc, s.r4a, s.r4b, s.r3b, s.r3a, s.r2))
             made.append(
                 Scatter(
                     p,
                     ref.at[piece(ci), :, :, :, :, :, lanes_of(ci)],
                     kind,
-                    lambda st, kind=kind: s.ss.at[st, kind, ci],
-                    lambda st, kind=kind: s.rs.at[st, kind, ci],
+                    lambda st, kind=kind: s.gs.at[st, kind],
+                    lambda st, kind=kind: s.gr.at[st, kind, ci],
                     bufs,
                 )
             )
@@ -1048,15 +1094,18 @@
     def k1(fs):
         for f in fs:
             f.t0_add()
-            f.t1_send()
+            f.t1a_send()
+
+    def k1b(fs):
+        for f in fs:
+            f.t1b_send()
 
     def k2(fs):
         for f in fs:
-            f.t1_add()
-
-        @pl.when(p.mid == 0)
-        def _():
-            for f in fs:
+            f.t1a_add()
+
+            @pl.when(p.mid == 0)
+            def _(f=f):
                 f.t2a_send()
 
     def k3(fs):
@@ -1067,12 +1116,13 @@
                 f.t2b_send()
 
     def k4(fs):
-        @pl.when(p.mid == 1)
-        def _():
-            for f in fs:
+        for f in fs:
+            f.t1b_add()
+
+            @pl.when(p.mid == 1)
+            def _(f=f):
                 f.t2b_add()
 
-        for f in fs:
             f.t3_send()
 
     first = p.zl == 0
@@ -1082,7 +1132,7 @@
         return jnp.where(first, top, low), jnp.where(first, low, top)
 
     def s1(ci):
-        return rcopy(s.st.at[ci], s.r1.at[ci], s.s1s.at[ci], s.s1r.at[ci], p.zdev)
+        return rcopy(s.st.at[ci], s.r1.at[ci], s.g1s.at[0], s.g1r.at[ci], p.zdev)
 
     def k5(ci):
         fa, fb = flows(ci)
@@ -1096,23 +1146,24 @@
         s1(ci).wait_recv()
         at = (piece(ci), ALL, lanes_of(ci))
         s.out[at] = s.out[at] + s.r1[ci].astype(F32)
-        for f in flows(ci):
-            f.drain()
-        s1(ci).wait_send()
+
+    def pack_of(fn):
+        return lambda ci: fn(flows(ci))
 
     stages = (
-        (0, lambda ci: k0(flows(ci))),
-        (1, lambda ci: k1(flows(ci))),
-        (2, lambda ci: k2(flows(ci))),
-        (4, lambda ci: k3(flows(ci))),
-        (6, lambda ci: k4(flows(ci))),
-        (8, k5),
-        (9, k6),
+        (0, 1, pack_of(k0)),
+        (S_K1, 1, pack_of(k1)),
+        (S_K1B, 1, pack_of(k1b)),
+        (S_K2, 1, pack_of(k2)),
+        (S_K3, 1, pack_of(k3)),
+        (S_K4, S_FAST, pack_of(k4)),
+        (S_K5, S_FAST, k5),
+        (S_K6, S_FAST, k6),
     )
     q = Scatter(
-        p, s.qg, 0, lambda st: s.qss.at[st], lambda st: s.qrs.at[st], (s.qc, s.q4, s.q3b, s.q3a, s.q2)
-    )
-    q1 = rcopy(s.qst, s.q1, s.qss.at[5], s.qrs.at[5], p.zdev)
+        p, s.qg, 0, lambda st: s.xs.at[st], lambda st: s.xr.at[st], (s.qc, s.q4a, s.q4b, s.q3b, s.q3a, s.q2)
+    )
+    q1 = rcopy(s.qst, s.q1, s.xs.at[6], s.xr.at[6], p.zdev)
 
     def q5():
         keep, give = halves(q.t3_sum())
@@ -1125,7 +1176,7 @@
         s.q_out[...] = s.q_out[...] + s.q1[:ROWS].astype(F32)
         q.drain()
 
-    query_steps = [lambda fn=fn: fn([q]) for fn in (k0, k1, k2, k3, k4)] + [q5, q6]
+    query_steps = [lambda fn=fn: fn([q]) for fn in (k0, k1, k1b, k2, k3, k4)] + [q5, q6]
     devs = (p.cdev, p.xdev, p.ydev, p.zdev, (p.b, (p.z + 2) % 4))
 
     def bcopy(k):
@@ -1143,15 +1194,23 @@
         else:
             s.bias_out[...] = total
 
-    return stages, query_steps, [lambda k=k: bias_step(k) for k in range(6)]
+    def drain():
+        for kind, ref in ((0, s.wa), (1, s.wb)):
+            sems = lambda st, kind=kind: s.gs.at[st, kind]
+            Scatter(p, ref, kind, sems, sems, (None,) * 6, (ALL,)).drain()
+        rcopy(s.st, s.r1, s.g1s.at[0], s.g1r.at[0], p.zdev).wait_send()
+
+    return stages, query_steps, [lambda k=k: bias_step(k) for k in range(6)], drain
 
 
 def run_stages(stages, t):
-    for off, fn in stages:
-
-        @pl.when((t >= off) & (t < NC + off))
-        def _(off=off, fn=fn):
-            fn(t - off)
+    for off, many, fn in stages:
+        for k in range(many):
+            ci = (t - off) * many + k
+
+            @pl.when((ci >= 0) & (ci < NC))
+            def _(ci=ci, fn=fn):
+                fn(ci)
 
 
 def run_at(t, table):
@@ -1170,15 +1229,28 @@
     p = Place()
     greet(p)
     me = p.b * 4 + p.z
-    vectors = Spread(p, s, s.small, 0, 32)
+    vectors = Spread(p, s, s.small, 0, 8)
     scores = Spread(p, s, s.sc, 1, 8)
-    s.small[pl.ds(pl.multiple_of(me * 32, 32), 32), :] = s.tile[...]
+    s.small[pl.ds(pl.multiple_of(me * 8, 8), 8), :] = s.tile[...]
     vectors.first()
-    stages = gather_steps(p, s)
-
-    def passages(fn, lo):
+    copies = {
+        name: pltpu.make_async_copy(src, dst, s.io.at[k])
+        for k, (name, src, dst) in enumerate(
+            (
+                ("x", s.x_in, s.x),
+                ("up", s.up_in, s.up),
+                ("lo", s.lo, s.lo_out),
+                ("hg", s.hg, s.hg_out),
+            )
+        )
+    }
+    copies["x"].start()
+    copies["up"].start()
+    stages, query_steps, drain = gather_steps(p, s)
+
+    def passages(fn, lo, many):
         def go():
-            pl.loop(lo, lo + 2)(lambda i: fn(s, i))
+            pl.loop(lo, lo + many)(lambda i: fn(s, i))
 
         return go
 
@@ -1186,51 +1258,59 @@
         vectors.finish()
         unpack_small(s)
 
-    forward = (
-        (3, vectors.second),
-        (7, small_done),
-        (9, lambda: qkv(s)),
-        (10, passages(attn_fwd, 0)),
-        (11, passages(attn_fwd, 2)),
-        (12, lambda: attn_out(s)),
-    )
-
-    @pl.loop(0, NC + 6)
+    ready = 2 * PARTS - 1 + G_END
+    forward = [
+        (1, copies["x"].wait),
+        (1, copies["up"].wait),
+        (2, vectors.second),
+        (6, small_done),
+        (ready, lambda: qkv(s)),
+        (ready + 1, passages(attn_fwd, 0, 2)),
+        (ready + 2, passages(attn_fwd, 2, 2)),
+        (ready + 3, lambda: attn_out(s)),
+    ]
+    forward += [(6 + 2 * k, fn) for k, fn in enumerate(query_steps)]
+    forward += [(15, lambda: unpack_queries(s))]
+
+    def ffn_until(t):
+        return jnp.minimum(jnp.maximum(2 * (t - ready - 3), 0), jnp.maximum(t - ready, 0))
+
+    @pl.loop(0, NC + G_END)
     def _(t):
         run_stages(stages, t)
         run_at(t, forward)
-
-        @pl.when((t >= 13) & (t <= 15))
-        def _():
-            ffn_fwd(s, t - 13)
-
-        @pl.when(t == 17)
-        def _():
-            ffn_fwd(s, 3)
-
+        pl.loop(ffn_until(t - 1), ffn_until(t))(lambda h: ffn_fwd(s, h))
+
+    drain()
     s.sc[pl.ds(pl.multiple_of(me * 8, 8), 8), :] = first_rows(s)
     scores.first()
     s.gv[...] = jnp.zeros_like(s.gv)
     norm2(s)
+    copies["lo"].start()
     scores.second()
     norm2_back(s)
     scores.finish()
     loss_part(s, me)
     add_cls(s)
 
-    stages, query_steps, bias_steps = scatter_steps(p, s)
+    stages, query_steps, bias_steps, drain = scatter_steps(p, s)
     ffn_back(s, 0)
+    def hidden():
+        qkv_back(s)
+        copies["hg"].start()
+
     backward = [
         (3, lambda: norm1_back(s)),
-        (4, passages(attn_back, 0)),
-        (5, passages(attn_back, 2)),
-        (6, lambda: qkv_back(s)),
-        (7, lambda: query_rows(s)),
+        (4, passages(attn_back, 0, 1)),
+        (5, passages(attn_back, 1, 1)),
+        (6, passages(attn_back, 2, 2)),
+        (7, hidden),
+        (8, lambda: query_rows(s)),
     ]
-    backward += [(8 + k, fn) for k, fn in enumerate(query_steps)]
-    backward += [(9 + 2 * k, fn) for k, fn in enumerate(bias_steps)]
-
-    @pl.loop(0, NC + 9)
+    backward += [(9 + k, fn) for k, fn in enumerate(query_steps)]
+    backward += [(8 + 2 * k, fn) for k, fn in enumerate(bias_steps)]
+
+    @pl.loop(0, S_END + 1)
     def _(t):
         run_stages(stages, t)
 
@@ -1240,18 +1320,22 @@
 
         run_at(t, backward)
 
-
-def layer(x, up, pack, tile):
+    drain()
+    copies["lo"].wait()
+    copies["hg"].wait()
+
+
+def layer(x, up, pack, tile, qpack):
     return pl.pallas_call(
         layer_kernel,
         out_shape=tuple(jax.ShapeDtypeStruct(*o) for o in OUTS.values()),
-        in_specs=[VM] * 4,
-        out_specs=(VM,) * len(OUTS),
+        in_specs=[HBM] * 2 + [VM] * 3,
+        out_specs=(HBM,) * 2 + (VM,) * 5,
         scratch_shapes=[pltpu.VMEM(*b) for b in SCRATCH.values()] + [DMA(n) for n in SEMS.values()],
         compiler_params=pltpu.CompilerParams(
             collective_id=1, has_side_effects=True, vmem_limit_bytes=VMEM_LIMIT
         ),
-    )(x, up, pack, tile)
+    )(x, up, pack, tile, qpack)
 
 
 def fast_local(
@@ -1278,7 +1362,7 @@
     second_shift,
 ):
     outer_t = outer_proj.T
-    pairs = [(value_proj, attn_proj.T), (query_proj, key_proj)]
+    pairs = [(query_proj, key_proj), (value_proj, attn_proj.T)]
     pairs += [(inner_proj[:, j * D : (j + 1) * D], outer_t[:, j * D : (j + 1) * D]) for j in range(4)]
     pack = jnp.stack([jnp.concatenate(pair, 0) for pair in pairs])
     vecs = jnp.stack(
@@ -1289,9 +1373,9 @@
         [positive_ids.T.astype(F32), positive_count[None].astype(F32), loss_weight[None], jnp.zeros((3, 4), F32)], 0
     )
     tile = jnp.concatenate([vecs, mid, aux, jnp.zeros((8, 4), F32)], 1)
-    tile = jnp.concatenate([tile, query_vectors.astype(F32).reshape(ROWS, 128)], 0)
+    qpack = jnp.concatenate([query_vectors.reshape(ROWS, 128), jnp.zeros((8, 128), BF)], 0)
     layer_output, hidden_grad, out, query_acc, bias, loss, cls_grad = layer(
-        hidden_in.reshape(TOK, D), upstream_grad.reshape(TOK, D), pack, tile
+        hidden_in.reshape(TOK, D), upstream_grad.reshape(TOK, D), pack, tile, qpack
     )
     me = lax.axis_index("blk") * 4 + lax.axis_index("grp")
     vec = lax.dynamic_slice(bias[:8], (0, ROWS * me), (8, ROWS))
@@ -1301,10 +1385,10 @@
         hidden_grad.reshape(hidden_in.shape),
         query_acc.reshape(4, D),
         lax.dynamic_slice(loss[0], (4 * me,), (4,)),
+        out[0, :ROWS],
+        out[0, ROWS:],
         out[1, :ROWS],
-        out[1, ROWS:],
-        out[0, :ROWS],
-        out[0, ROWS:].T,
+        out[1, ROWS:].T,
         vec[0],
         vec[1],
         vec[2],

time: 198 us -> 177 us (0.89)
  Pallas kernels: 179 us -> 157 us
  other arithmetic: 4.21 us -> 2.19 us
    pallas_call x1, Pallas kernels: 179 us -> 157 us  [layer(): pl.pallas_call(layer_kernel, out_shape=tuple((jax.ShapeDtypeStruct(*o) fo...]
    unnamed x21 -> x45, local copies, waits for them, and re-layouts: 4.6 us -> 7.2 us
where the time goes in v2:
time: 177 us; the launch traced here: 176 us
  Pallas kernels  157 us (89%)
  local copies, waits for them, and re-layouts  16 us (9%)
  other arithmetic  2.19 us (1%)
    pallas_call x1, Pallas kernels, layer(): pl.pallas_call(layer_kernel, out_shape=tuple((jax.ShapeDtypeStruct(*o) fo...  157 us
    unnamed x45, local copies, waits for them, and re-layouts  7.2 us

profile of v2, /device:TPU:0, one launch (start us, length us, event | category | flops | bytes accessed | tf_op | source)
XLA Modules:
  0.0 176.3 jit_solution(3961424174127000323)
XLA Ops:
  0.7 0.0 copy-start.20
  0.7 0.6 copy-done.20
  1.3 0.0 copy-start.9
  1.3 0.1 pad.19.clone
  1.4 0.6 copy-done.9
  2.0 0.1 copy.41
  2.1 0.0 copy-start.10
  2.1 0.0 copy-start.11
  2.1 0.0 copy-start.12
  2.1 0.0 copy-start.13
  2.1 0.0 copy-start.14
  2.1 0.0 copy-start.15
  2.1 0.0 copy-start.16
  2.1 0.0 copy-start.17
  2.2 0.6 copy-done.10
  2.8 0.0 copy-done.11
  2.8 0.0 copy-done.12
  2.8 0.0 copy-done.13
  2.8 0.0 copy-done.14
  2.8 0.0 copy-done.15
  2.8 0.0 copy-done.16
  2.8 0.0 copy-done.17
  2.9 0.0 copy-start.18
  2.9 0.6 copy-done.18
  3.6 0.0 copy-start.19
  3.6 0.6 copy-done.19
  4.2 0.0 copy-start.8
  4.2 0.7 maximum_maximum_fusion.refs_3_
  4.9 0.0 copy-done.8
  4.9 0.6 concatenate.43.refs_4_
  5.5 0.0 copy-start.3
  5.5 0.0 copy-start.4
  5.5 0.9 fusion.6
  6.5 0.0 copy-done.3
  6.5 0.0 copy-done.4
  6.5 0.0 copy-start.5
  6.5 0.0 copy-start.6
  6.5 0.7 copy-done.5
  7.2 0.0 copy-done.6
  7.3 0.0 copy-start.2
  7.3 0.8 copy-done.2
  8.1 157.2 %shard_map.356 = (bf16[512,768]{1,0:T(8,128)(2,1)}, bf16[512,768]{1,0:T(8,128)(2,1)}, f32[6,48,768]{2,1,0:T(8,128)}, f32[24,128]{1,0:T(8,128)}, f32[16,768]{1,0:...) custom-call(bf16[512,768]{1,0:T(8,128)(2,1)} %bitcast.92, bf16[512,768]{1,0:T(8,128)(2,1)} %bitcast.93, ...), custom_call_target="tpu_custom_call" | custom-call | tf_op jit(solution)/shard_map/pallas_call | solution.py:1329
  165.3 0.0 copy-start.7
  165.4 0.7 slice.118
  166.0 0.6 dynamic-slice_bitcast_fusion
  166.6 1.3 reshape.98
  167.9 1.3 slice.141
  169.3 0.0 copy-done.7
  169.3 0.1 constant_dynamic-slice_fusion
  169.4 0.6 dynamic_slice.14
  170.0 0.5 slice_bitcast_fusion.12
  170.5 2.0 %slice_bitcast_fusion.3 = (f32[24,768]{1,0:T(8,128)S(1)}, f32[24,768]{1,0:T(8,128)S(1)}, f32[24,768]{1,0:T(8,128)S(1)}, f32[24,768]{1,0:T(8,128)S(1)}, f32[24,76...) fusion(f32[6,48,768]{2,1,0:T(8,128)} %get-tuple-element.43), kind=kLoop, calls=%fused_computation.17 | loop fusion | bytes 1769472 | tf_op jit(solution)/shard_map/squeeze | solution.py:1399
  172.5 0.0 copy-start.1
  172.5 0.7 maximum_bitcast_fusion
  173.2 0.7 pad_maximum_fusion
  174.0 0.0 copy-done.1
  174.0 0.0 copy-start
  174.0 0.9 copy.49
  174.8 0.5 copy-done
  175.4 0.9 copy.50
  (17 shorter events, 0.1 us)
Async XLA Ops:
  0.7 0.7 copy-start.20
  1.3 0.7 copy-start.9
  2.1 0.7 copy-start.10
  2.1 0.7 copy-start.11
  2.1 0.7 copy-start.12
  2.1 0.7 copy-start.13
  2.1 0.7 copy-start.14
  2.1 0.7 copy-start.15
  2.1 0.7 copy-start.16
  2.1 0.7 copy-start.17
  2.9 0.7 copy-start.18
  3.6 0.7 copy-start.19
  4.2 0.7 copy-start.8
  5.5 0.9 copy-start.3
  5.5 0.9 copy-start.4
  6.5 0.8 copy-start.5
  6.5 0.8 copy-start.6
  7.3 0.8 copy-start.2
  165.3 3.9 %copy-start.7 = (f32[16,768]{1,0:T(8,128)S(1)}, f32[16,768]{1,0:T(8,128)}, u32[]{:S(2)}) copy-start(f32[16,768]{1,0:T(8,128)} %get-tuple-element.44) | copy-start | bytes 147460
  172.5 1.5 copy-start.1
  174.0 1.4 copy-start

commit v3 on v2

--- a/solution.py
+++ b/solution.py
@@ -721,6 +721,37 @@
     return hot, owner[0:1]
 
 
+def pack_weights(s, i):
+    if i == 0:
+        top, low = s.w_query[...].astype(F32), s.w_key[...].astype(F32)
+    elif i == 1:
+        top, low = s.w_value[...].astype(F32), s.w_attn[...].astype(F32)
+    else:
+        at = slice((i - 2) * D, (i - 1) * D)
+        top, low = s.w_inner[:, at].astype(F32), s.w_outer[:, at].astype(F32)
+    s.pack[i] = jnp.concatenate([top, low], 0).astype(BF)
+
+
+def pack_small(s):
+    for t, name in enumerate(VECTORS[:8]):
+        s.tile[t : t + 1, 0:ROWS] = getattr(s, name)[...].astype(F32).reshape(1, ROWS)
+    row = lax.broadcasted_iota(jnp.int32, (8, 128), 0)
+    lane = lax.broadcasted_iota(jnp.int32, (8, 128), 1)
+    tile = jnp.where(lane < ROWS, s.tile[...], 0.0)
+    inner = s.inner_bias[...].astype(F32).reshape(1, 96)
+    inner = pltpu.roll(jnp.concatenate([inner, jnp.zeros((1, 32), F32)], 1), ROWS, 1)
+    tile = jnp.where((row == 0) & (lane >= ROWS) & (lane < ROWS + 96), inner, tile)
+    for q in range(4):
+        values = [s.positive_ids[q, k].astype(F32) for k in range(3)]
+        values += [s.positive_count[q].astype(F32), s.loss_weight[q]]
+        for t, value in enumerate(values):
+            tile = jnp.where((row == t) & (lane == 120 + q), value, tile)
+    queries = s.w_queries[...].astype(F32)
+    rows = [queries[q : q + 1, k * 128 : (k + 1) * 128] for q in range(4) for k in range(6)]
+    s.qpack[...] = jnp.concatenate(rows + [jnp.zeros((8, 128), F32)], 0).astype(BF)
+    return tile
+
+
 def unpack_small(s):
     sm = s.small[...]
     hot, owner = column_maps(24, 0, 0.0)
@@ -841,11 +872,25 @@
     loss=((8, 128), F32),
     cgrad=((8, D), F32),
 )
-INS = ("x_in", "up_in", "pack", "tile", "qpack")
+VECTORS = (
+    "query_bias",
+    "value_bias",
+    "attn_bias",
+    "first_gain",
+    "first_shift",
+    "outer_bias",
+    "second_gain",
+    "second_shift",
+    "inner_bias",
+)
+INS = ("x_in", "up_in") + ("w_query", "w_key", "w_value", "w_attn", "w_inner", "w_outer", "w_queries") + VECTORS
+INS += ("loss_weight", "positive_ids", "positive_count")
 SCRATCH = dict(
     wa=((6, 2, 2, 2, 2, 48, D), BF),
     wb=((6, 2, 2, 2, 2, 48, D), BF),
     rb=((6, 48, D), BF),
+    pack=((6, 48, D), BF),
+    qpack=((32, 128), BF),
     x=((TOK, D), BF),
     up=((TOK, D), BF),
     lo=((TOK, D), BF),
@@ -865,6 +910,7 @@
     bg=((TOK, D), BF),
     tmp=((TOK, D), F32),
     small=((256, 128), F32),
+    tile=((8, 128), F32),
     qx=((2, 2, 2, 2, 48, 128), BF),
     qrb=((32, 128), BF),
     sc=((256, 128), F32),
@@ -953,7 +999,7 @@
             self.bcopy(k, self.bview(self.p.b)).wait_send()
 
 
-def gather_steps(p, s):
+def gather_steps(p, s, me, vectors):
     def flows(ci):
         out = []
         for kind, ref in ((0, s.wa), (1, s.wb)):
@@ -1033,10 +1079,13 @@
         rcopy(s.pack, s.rb, s.g1s.at[0], s.g1r.at[0], p.zdev).wait_send()
         q.drain()
 
-    @pl.loop(0, NC)
-    def _(ci):
-        s1(ci).start()
-
+    for i in range(6):
+        pack_weights(s, i)
+        for h in range(PARTS):
+            s1(PARTS * i + h).start()
+
+    s.small[pl.ds(pl.multiple_of(me * 8, 8), 8), :] = pack_small(s)
+    vectors.first()
     q = Gather(p, s.qx, 0, lambda st: s.xs.at[st], lambda st: s.xr.at[st])
     q1 = rcopy(s.qpack, s.qrb, s.xs.at[7], s.xr.at[7], p.zdev)
     q1.start()
@@ -1231,8 +1280,6 @@
     me = p.b * 4 + p.z
     vectors = Spread(p, s, s.small, 0, 8)
     scores = Spread(p, s, s.sc, 1, 8)
-    s.small[pl.ds(pl.multiple_of(me * 8, 8), 8), :] = s.tile[...]
-    vectors.first()
     copies = {
         name: pltpu.make_async_copy(src, dst, s.io.at[k])
         for k, (name, src, dst) in enumerate(
@@ -1246,7 +1293,7 @@
     }
     copies["x"].start()
     copies["up"].start()
-    stages, query_steps, drain = gather_steps(p, s)
+    stages, query_steps, drain = gather_steps(p, s, me, vectors)
 
     def passages(fn, lo, many):
         def go():
@@ -1310,7 +1357,7 @@
     backward += [(9 + k, fn) for k, fn in enumerate(query_steps)]
     backward += [(8 + 2 * k, fn) for k, fn in enumerate(bias_steps)]
 
-    @pl.loop(0, S_END + 1)
+    @pl.loop(0, max(S_END, 18) + 1)
     def _(t):
         run_stages(stages, t)
 
@@ -1325,17 +1372,64 @@
     copies["hg"].wait()
 
 
-def layer(x, up, pack, tile, qpack):
+SMEM = pl.BlockSpec(memory_space=pltpu.SMEM)
+
+
+def layer(*args):
     return pl.pallas_call(
         layer_kernel,
         out_shape=tuple(jax.ShapeDtypeStruct(*o) for o in OUTS.values()),
-        in_specs=[HBM] * 2 + [VM] * 3,
+        in_specs=[HBM] * 2 + [VM] * (len(INS) - 5) + [SMEM] * 3,
         out_specs=(HBM,) * 2 + (VM,) * 5,
         scratch_shapes=[pltpu.VMEM(*b) for b in SCRATCH.values()] + [DMA(n) for n in SEMS.values()],
         compiler_params=pltpu.CompilerParams(
             collective_id=1, has_side_effects=True, vmem_limit_bytes=VMEM_LIMIT
         ),
-    )(x, up, pack, tile, qpack)
+    )(*args)
+
+
+def finish_kernel(
+    out, q_out, bias, loss, cgrad,
+    query_grad, query_loss, g_query, g_key, g_value, g_attn,
+    g_qb, g_vb, g_ab, g_fg, g_fs, g_inner, g_ib, g_outer, g_ob, g_sg, g_ss, cls_grad
+):
+    me = lax.axis_index("blk") * 4 + lax.axis_index("grp")
+    for q in range(4):
+        for k in range(6):
+            query_grad[q : q + 1, k * 128 : (k + 1) * 128] = q_out[6 * q + k : 6 * q + k + 1, :]
+    cls_grad[...] = cgrad[0:4, :]
+    g_query[...] = out[0, :ROWS]
+    g_key[...] = out[0, ROWS:]
+    g_value[...] = out[1, :ROWS]
+    g_attn[...] = out[1, ROWS:]
+    for j in range(4):
+        at = slice(j * D, (j + 1) * D)
+        g_inner[:, at] = out[2 + j, :ROWS]
+        g_outer[:, at] = out[2 + j, ROWS:]
+    wide = pltpu.roll(bias[0:8, :], lax.rem(D - ROWS * me, D), 1)
+    for t, ref in enumerate((g_qb, g_vb, g_ab, g_fg, g_fs, g_ob, g_sg, g_ss)):
+        ref[...] = wide[t, :ROWS]
+    group = me // 8
+    inner = jnp.sum(jnp.where(lax.broadcasted_iota(jnp.int32, (8, D), 0) == group, bias[8:16, :], 0.0), axis=0, keepdims=True)
+    inner = jnp.broadcast_to(inner, (8, D))
+    inner = pltpu.roll(inner, lax.rem(D - 96 * lax.rem(me, 8), D), 1)
+    g_ib[...] = inner[0, :96]
+    query_loss[...] = pltpu.roll(loss[...], lax.rem(128 - 4 * me, 128), 1)[0, :4]
+
+
+def finish(*args):
+    f32 = lambda *dims: jax.ShapeDtypeStruct(dims, F32)
+    square = f32(ROWS, D)
+    vec = f32(ROWS)
+    outs = [f32(4, D), f32(4)] + [square] * 4 + [vec] * 5
+    outs += [f32(ROWS, 4 * D), f32(96), f32(ROWS, 4 * D), vec, vec, vec, f32(4, D)]
+    return pl.pallas_call(
+        finish_kernel,
+        out_shape=outs,
+        in_specs=[VM] * 5,
+        out_specs=[VM] * 18,
+        compiler_params=pltpu.CompilerParams(vmem_limit_bytes=VMEM_LIMIT),
+    )(*args)
 
 
 def fast_local(
@@ -1361,47 +1455,34 @@
     second_gain,
     second_shift,
 ):
-    outer_t = outer_proj.T
-    pairs = [(query_proj, key_proj), (value_proj, attn_proj.T)]
-    pairs += [(inner_proj[:, j * D : (j + 1) * D], outer_t[:, j * D : (j + 1) * D]) for j in range(4)]
-    pack = jnp.stack([jnp.concatenate(pair, 0) for pair in pairs])
-    vecs = jnp.stack(
-        [query_bias, value_bias, attn_bias, first_gain, first_shift, outer_bias, second_gain, second_shift]
-    ).astype(F32)
-    mid = jnp.zeros((8, 96), F32).at[0].set(inner_bias.astype(F32))
-    aux = jnp.concatenate(
-        [positive_ids.T.astype(F32), positive_count[None].astype(F32), loss_weight[None], jnp.zeros((3, 4), F32)], 0
-    )
-    tile = jnp.concatenate([vecs, mid, aux, jnp.zeros((8, 4), F32)], 1)
-    qpack = jnp.concatenate([query_vectors.reshape(ROWS, 128), jnp.zeros((8, 128), BF)], 0)
-    layer_output, hidden_grad, out, query_acc, bias, loss, cls_grad = layer(
-        hidden_in.reshape(TOK, D), upstream_grad.reshape(TOK, D), pack, tile, qpack
-    )
-    me = lax.axis_index("blk") * 4 + lax.axis_index("grp")
-    vec = lax.dynamic_slice(bias[:8], (0, ROWS * me), (8, ROWS))
-    inner_vec = lax.dynamic_slice(bias[8:12].reshape(-1), (96 * me,), (96,))
-    return (
-        layer_output.reshape(hidden_in.shape),
-        hidden_grad.reshape(hidden_in.shape),
-        query_acc.reshape(4, D),
-        lax.dynamic_slice(loss[0], (4 * me,), (4,)),
-        out[0, :ROWS],
-        out[0, ROWS:],
-        out[1, :ROWS],
-        out[1, ROWS:].T,
-        vec[0],
-        vec[1],
-        vec[2],
-        vec[3],
-        vec[4],
-        jnp.concatenate([out[j, :ROWS] for j in range(2, 6)], 1),
-        inner_vec,
-        jnp.concatenate([out[j, ROWS:] for j in range(2, 6)], 1).T,
-        vec[5],
-        vec[6],
-        vec[7],
-        cls_grad[:4],
-    )
+    results = layer(
+        hidden_in.reshape(TOK, D),
+        upstream_grad.reshape(TOK, D),
+        query_proj,
+        key_proj,
+        value_proj,
+        attn_proj.T,
+        inner_proj,
+        outer_proj.T,
+        query_vectors,
+        query_bias,
+        value_bias,
+        attn_bias,
+        first_gain,
+        first_shift,
+        outer_bias,
+        second_gain,
+        second_shift,
+        inner_bias,
+        loss_weight,
+        positive_ids,
+        positive_count,
+    )
+    layer_output, hidden_grad = (part.reshape(hidden_in.shape) for part in results[:2])
+    rest = list(finish(*results[2:]))
+    rest[5] = rest[5].T
+    rest[13] = rest[13].T
+    return (layer_output, hidden_grad, *rest)
 
 
 def solution(mesh):

time: 177 us -> 165 us (0.932)
  local copies, waits for them, and re-layouts: 16 us -> 2.29 us
  Pallas kernels: 157 us -> 161 us
  other arithmetic: 2.19 us -> 0 us
    unnamed x45 -> x6, local copies, waits for them, and re-layouts: 7.2 us -> 2.29 us
    slice x5 -> x0, local copies, waits for them, and re-layouts: 2.95 us -> none  [the longest x1 1.34 us: fast_local(): cls_grad[:4]]
    squeeze x2 -> x0, local copies, waits for them, and re-layouts: 2.53 us -> none  [the longest x1 1.99 us: fast_local(): out[j, ROWS:]]
    pallas_call x0 -> x1, Pallas kernels: none -> 2.25 us  [finish(): pl.pallas_call(finish_kernel, out_shape=outs, in_specs=[VM] * 5, out_spec...]
    pallas_call x1, Pallas kernels: 157 us -> 159 us  [layer(): pl.pallas_call(layer_kernel, out_shape=tuple((jax.ShapeDtypeStruct(*o) fo...]
where the time goes in v3:
time: 165 us; the launch traced here: 164 us
  Pallas kernels  161 us (98%)
  local copies, waits for them, and re-layouts  2.29 us (1%)
    pallas_call x1, Pallas kernels, layer(): pl.pallas_call(layer_kernel, out_shape=tuple((jax.ShapeDtypeStruct(*o) fo...  159 us

profile of v3, /device:TPU:0, one launch (start us, length us, event | category | flops | bytes accessed | tf_op | source)
XLA Modules:
  0.0 164.5 jit_solution(15726355758900672293)
XLA Ops:
  0.7 159.2 %shard_map.356 = (bf16[512,768]{1,0:T(8,128)(2,1)}, bf16[512,768]{1,0:T(8,128)(2,1)}, f32[6,48,768]{2,1,0:T(8,128)}, f32[24,128]{1,0:T(8,128)}, f32[16,768]{1,0:...) custom-call(bf16[512,768]{1,0:T(8,128)(2,1)} %bitcast.8, bf16[512,768]{1,0:T(8,128)(2,1)} %bitcast.9, ...), custom_call_target="tpu_custom_call" | custom-call | tf_op jit(solution)/shard_map/pallas_call | solution.py:1379
  159.9 0.0 copy-start.1
  159.9 2.3 %shard_map.357 = (f32[4,768]{1,0:T(4,128)}, f32[4]{0:T(128)}, f32[24,768]{1,0:T(8,128)}, f32[24,768]{1,0:T(8,128)}, f32[24,768]{1,0:T(8,128)}, /*index=5*/f32[24...) custom-call(f32[6,48,768]{2,1,0:T(8,128)} %get-tuple-element.47.out,, ...), custom_call_target="tpu_custom_call" | custom-call | tf_op jit(solution)/shard_map/pallas_call | solution.py:1426
  162.2 0.0 copy-done.1
  162.2 0.0 copy-start
  162.2 0.9 copy.43
  163.1 0.5 copy-done
  163.6 0.9 copy.44
Async XLA Ops:
  159.9 2.3 %copy-start.1 = (bf16[512,768]{1,0:T(8,128)(2,1)S(1)}, bf16[512,768]{1,0:T(8,128)(2,1)}, u32[]{:S(2)}) copy-start(bf16[512,768]{1,0:T(8,128)(2,1)} %get-tuple-element.45) | copy-start | bytes 2359300
  162.2 1.4 copy-start

commit v4 on v3

--- a/solution.py
+++ b/solution.py
@@ -492,7 +492,7 @@
     def add(self, stage, buf, f, s, zz):
         self.copy(stage, buf, buf, self.p.cdev).wait_recv()
         at = self.index(f, s, zz, self.p.c)
-        self.ref[at] = (self.ref[at].astype(F32) + buf[...].astype(F32)).astype(BF)
+        self.ref[at] = self.ref[at] + buf[...]
 
     def t0_send(self):
         self.copy(0, self.at(ALL, ALL, ALL, 1 - self.p.c), self.rc, self.p.cdev).start()
@@ -565,11 +565,15 @@
     lo = (lane < 64).astype(F32).astype(BF)
     return lo, (1 - lo.astype(F32)).astype(BF)
 
-def qkv(s):
+def queries_keys(s):
     x = s.x[...]
     s.q[...] = ((nn(x, weight(s.wa, 0)) + s.vec[0:1, :]) * 0.125).astype(BF)
     s.k[...] = nn(x, weight(s.wb, 0)).astype(BF)
-    s.v[...] = (nn(x, weight(s.wa, 1)) + s.vec[1:2, :]).astype(BF)
+
+
+def values(s):
+    s.v[...] = (nn(s.x[...], weight(s.wa, 1)) + s.vec[1:2, :]).astype(BF)
+
 
 def split(x, lo, hi): return jnp.concatenate([x * lo, x * hi], 0)
 
@@ -611,10 +615,10 @@
     phi = jnp.where(x > 0, 1.0 - half, half)
     return phi, e * 0.3989422804014327
 
-def ffn_fwd(s, h):
-    j, ln = h // PARTS, lanes_of(h)
-    w_in = s.wa[2 + j, :, :, :, :, :, ln].reshape(D, LW)
-    w_out = s.wb[2 + j, :, :, :, :, :, ln].reshape(D, LW)
+def ffn_fwd(s, j, h, width):
+    ln = pl.ds(pl.multiple_of(h * width, 128), width) if width < D else ALL
+    w_in = s.wa[2 + j, :, :, :, :, :, ln].reshape(D, width)
+    w_out = s.wb[2 + j, :, :, :, :, :, ln].reshape(D, width)
     for r in (slice(0, 256), slice(256, 512)):
         x = nn(s.nl[r, :], w_in) + s.vec[pl.ds(8 + j, 1), ln]
         cdf, pdf = gelu_parts(x)
@@ -650,16 +654,26 @@
         s.gv[5] += colsum(b.astype(F32))
     tiles(2, body)
 
-def ffn_back(s, j):
+def outer_back(s, j):
     s.tmp[...] = nn(s.bg[...], weight(s.wb, 2 + j))
     keep(s.wb, 2 + j, tn(s.bg[...], s.act[j]))
+
+
+def inner_back(s, j):
     def ew(r):
         ig = (s.tmp[r, :] * s.gp[j, r, :].astype(F32)).astype(BF)
         s.gp[j, r, :] = ig
         s.gv[8 + j] += colsum(ig.astype(F32))
+
     tiles(2, ew)
     s.acc[...] += nt(s.gp[j], weight(s.wa, 2 + j))
     keep(s.wa, 2 + j, tn(s.nl[...], s.gp[j]))
+
+
+def ffn_back(s, j):
+    outer_back(s, j)
+    inner_back(s, j)
+
 
 def norm1_back(s):
     def body(r):
@@ -786,13 +800,17 @@
     return jnp.concatenate([s.qm[k * 128 : (k + 1) * 128, :] for k in range(6)], 1).astype(BF)
 
 
-def first_rows(s):
+def first_rows(s, me):
     rows = [s.acc[p * LEN : p * LEN + 8, :][0:1] for p in range(4)]
     n_, inv = normalize(jnp.concatenate(rows + [jnp.zeros((4, D), F32)], 0))
     s.cn[...] = n_
     s.ci[...] = inv
     cls = (n_ * s.vec[6:7, :] + s.vec[7:8, :]).astype(BF)
-    s.cls[...] = cls.astype(F32)
+    low = cls.astype(F32)
+    s.cls[...] = low
+    parts = [low[0:4, k * 256 : (k + 1) * 256] for k in range(3)]
+    tile = jnp.concatenate(parts + [jnp.zeros((4, 256), F32)], 0).astype(BF)
+    s.call[pl.ds(pl.multiple_of(me * 16, 16), 16), :] = tile
     return nt(cls, all_queries(s))
 
 
@@ -820,24 +838,32 @@
         totals.append(top + jnp.log(jnp.sum(jnp.exp(part - top), axis=0, keepdims=True)))
     total_all, total_pos = totals
     s.loss[...] = jnp.broadcast_to(total_all - total_pos, (8, 128))
-    own = s.sc[pl.ds(pl.multiple_of(me * 8, 8), 8), :]
-    slot = lax.broadcasted_iota(jnp.int32, (8, 128), 0)
-    hit = hits((4 * me + slot).astype(F32))
-    pull = jnp.where(hit, jnp.exp(own - total_pos), 0.0)
-    grad = weight_q * (jnp.exp(own - total_all) - pull)
-    grad = jnp.where(slot < 4, grad, 0.0).astype(BF)
-    s.cgrad[...] = nn(grad, all_queries(s))
-    part = tn(grad, s.cls[...].astype(BF))
-    for k in range(6):
-        s.qpart[k * 128 : (k + 1) * 128, :] = part[:, k * 128 : (k + 1) * 128]
-
-
-def query_rows(s):
-    for q in range(4):
-        for k in range(6):
-            piece = s.qpart[pl.ds(k * 128 + q, 32, stride=4), :]
-            s.qrow[pl.ds(6 * q + k, 32, stride=24), :] = piece
-    s.qg[...] = s.qrow[...].astype(BF).reshape(2, 2, 2, 2, 48, 128)
+    pull = jnp.where(hits(passage) & real, jnp.exp(scores - total_pos), 0.0)
+    grad = jnp.where(real, weight_q * (jnp.exp(jnp.where(real, scores - total_all, 0.0)) - pull), 0.0)
+    s.sg[...] = grad
+    own = s.sg[pl.ds(pl.multiple_of(me * 8, 8), 8), :].astype(BF)
+    s.cgrad[...] = nn(own, all_queries(s))
+
+
+def query_gradient(s, me):
+    own = pltpu.roll(s.sg[...], lax.rem(128 - 4 * me, 128), 1).reshape(32, 8, 128)[:, :4]
+    vectors = s.call[...]
+    for k in range(3):
+        pieces = [jnp.zeros((32, 4, 128), F32)] * k + [own] + [jnp.zeros((32, 4, 128), F32)] * (3 - k)
+        grad = jnp.concatenate(pieces, 1).reshape(512, 128).astype(BF)
+        s.q_out[:, k * 256 : (k + 1) * 256] = tn(grad, vectors)[0:8]
+
+
+def pack_vectors(s):
+    vec = jnp.sum(s.gv[...], axis=1)
+    first = lax.broadcasted_iota(jnp.int32, (8, 96), 0) == 0
+    for dev in range(32):
+        b, z = dev // 4, dev % 4
+        wide = vec[0:8, ROWS * dev : ROWS * (dev + 1)]
+        at = 96 * (dev % 8)
+        inner = jnp.where(first, vec[8 + dev // 8 : 9 + dev // 8, at : at + 96], 0.0)
+        tile = jnp.concatenate([inner, wide, jnp.zeros((8, 8), F32)], 1)
+        s.pb[(z * 8 + b) * 8 : (z * 8 + b + 1) * 8, :] = tile
 
 
 def add_cls(s):
@@ -859,16 +885,30 @@
 
 
 HBM = pl.BlockSpec(memory_space=pl.ANY)
-MERGES, G_S23, G_S4A, G_S34, G_S45, G_END = 2, 1, 2, 3, 5, 6
-S_K1, S_K1B, S_K2, S_K3, S_K4, S_K5, S_K6 = 1, 3, 2, 3, 10, 11, 12
-S_FAST = 2
-S_END = S_K6 + NC // S_FAST
+G_MERGE = ((0, 2, NC),)
+G_S23 = ((1, 1, NC),)
+G_S4A = ((3, 1, NC),)
+G_S34 = ((3, 1, NC),)
+G_S45 = ((5, 1, NC),)
+G_CORE = ((6, 1, NC),)
+G_FULL = ((12, 1, 2), (15, 1, 1))
+G_HALF = ((16, 1, 2),)
+G_END = 18
+S_K0 = ((0, 2, 8), (9, 2, 4))
+S_K1 = ((1, 2, 8), (11, 2, 4))
+S_K1B = ((2, 1, 8), (13, 2, 4))
+S_K2 = ((2, 1, 8), (12, 2, 4))
+S_K3 = ((4, 1, NC),)
+S_K4 = ((11, 2, NC),)
+S_K5 = ((12, 2, NC),)
+S_K6 = ((15, 2, NC),)
+S_END = 21
 OUTS = dict(
     lo_out=((TOK, D), BF),
     hg_out=((TOK, D), BF),
     out=((6, 48, D), F32),
-    q_out=((ROWS, 128), F32),
-    bias_out=((16, D), F32),
+    q_out=((8, D), F32),
+    bias_out=((8, 128), F32),
     loss=((8, 128), F32),
     cgrad=((8, D), F32),
 )
@@ -921,9 +961,7 @@
     cn=((8, D), F32),
     ci=((8, 1), F32),
     cls=((8, D), F32),
-    qpart=((D, 128), F32),
     qrow=((D, 128), F32),
-    qg=((2, 2, 2, 2, 48, 128), BF),
     rc=((2, NC, 2, 2, 2, 48, LW), BF),
     r4a=((2, NC, 2, 48, LW), BF),
     r4b=((2, NC, 2, 48, LW), BF),
@@ -932,16 +970,12 @@
     r2=((2, NC, 48, LW), BF),
     st=((NC, 48, LW), BF),
     r1=((NC, 48, LW), BF),
-    qc=((2, 2, 2, 48, 128), BF),
-    q4a=((2, 48, 128), BF),
-    q4b=((2, 48, 128), BF),
-    q3b=((2, 48, 128), BF),
-    q3a=((2, 48, 128), BF),
-    q2=((48, 128), BF),
-    qst=((32, 128), BF),
-    q1=((32, 128), BF),
-    bs_buf=((5, 16, D), F32),
-    br_buf=((5, 16, D), F32),
+    call=((512, 256), BF),
+    sg=((256, 128), F32),
+    pb=((256, 128), F32),
+    zb=((4, 64, 128), F32),
+    bb=((8, 8, 128), F32),
+    half=((64, 128), F32),
 )
 SEMS = dict(
     gs=(7, 2),
@@ -950,12 +984,10 @@
     g1r=(NC,),
     xs=(8,),
     xr=(8,),
-    bss=(5,),
-    brs=(5,),
-    zs=(2, 4),
-    zr=(2, 4),
-    bs=(2, 8),
-    br=(2, 8),
+    zs=(4, 4),
+    zr=(4, 4),
+    bs=(4, 8),
+    br=(4, 8),
     io=(4,),
 )
 
@@ -1106,12 +1138,12 @@
         return lambda ci: fn(flows(ci))
 
     stages = (
-        (0, MERGES, merge),
-        (G_S23, 1, pack_of(s23)),
-        (G_S4A, 1, pack_of(s4a)),
-        (G_S34, 1, pack_of(s34)),
-        (G_S45, 1, pack_of(s45)),
-        (G_END, 1, pack_of(core)),
+        (G_MERGE, merge),
+        (G_S23, pack_of(s23)),
+        (G_S4A, pack_of(s4a)),
+        (G_S34, pack_of(s34)),
+        (G_S45, pack_of(s45)),
+        (G_CORE, pack_of(core)),
     )
     return stages, query_steps, drain
 
@@ -1136,9 +1168,15 @@
             )
         return made
 
-    def k0(fs):
-        for f in fs:
-            f.t0_send()
+    def k0(ci):
+        @pl.when(ci >= PARTS)
+        def _():
+            for f in flows(ci):
+                f.t0_send()
+
+    def early(kind):
+        for ci in range(PARTS):
+            flows(ci)[kind].t0_send()
 
     def k1(fs):
         for f in fs:
@@ -1200,48 +1238,45 @@
         return lambda ci: fn(flows(ci))
 
     stages = (
-        (0, 1, pack_of(k0)),
-        (S_K1, 1, pack_of(k1)),
-        (S_K1B, 1, pack_of(k1b)),
-        (S_K2, 1, pack_of(k2)),
-        (S_K3, 1, pack_of(k3)),
-        (S_K4, S_FAST, pack_of(k4)),
-        (S_K5, S_FAST, k5),
-        (S_K6, S_FAST, k6),
-    )
-    q = Scatter(
-        p, s.qg, 0, lambda st: s.xs.at[st], lambda st: s.xr.at[st], (s.qc, s.q4a, s.q4b, s.q3b, s.q3a, s.q2)
-    )
-    q1 = rcopy(s.qst, s.q1, s.xs.at[6], s.xr.at[6], p.zdev)
-
-    def q5():
-        keep, give = halves(q.t3_sum())
-        s.qst[...] = jnp.concatenate([give, jnp.zeros((8, 128), F32)], 0).astype(BF)
-        q1.start()
-        s.q_out[...] = keep
-
-    def q6():
-        q1.wait()
-        s.q_out[...] = s.q_out[...] + s.q1[:ROWS].astype(F32)
-        q.drain()
-
-    query_steps = [lambda fn=fn: fn([q]) for fn in (k0, k1, k1b, k2, k3, k4)] + [q5, q6]
-    devs = (p.cdev, p.xdev, p.ydev, p.zdev, (p.b, (p.z + 2) % 4))
+        (S_K0, k0),
+        (S_K1, pack_of(k1)),
+        (S_K1B, pack_of(k1b)),
+        (S_K2, pack_of(k2)),
+        (S_K3, pack_of(k3)),
+        (S_K4, pack_of(k4)),
+        (S_K5, k5),
+        (S_K6, k6),
+    )
+    def zcopy(k):
+        dz = (p.z + k) % 4
+        src = s.pb.at[pl.ds(pl.multiple_of(dz * 64, 64), 64), :]
+        return rcopy(src, s.zb.at[k], s.zs.at[3, k], s.zr.at[3, k], (p.b, dz))
 
     def bcopy(k):
-        return rcopy(s.bs_buf.at[k], s.br_buf.at[k], s.bss.at[k], s.brs.at[k], devs[k])
-
-    def bias_step(k):
-        if k == 0:
-            total = jnp.concatenate([jnp.sum(s.gv[...], axis=1), jnp.zeros((4, D), F32)], 0)
-        else:
-            bcopy(k - 1).wait()
-            total = s.bs_buf[k - 1] + s.br_buf[k - 1]
-        if k < 5:
-            s.bs_buf[k] = total
+        db = (p.b + k) % 8
+        src = s.half.at[pl.ds(pl.multiple_of(db * 8, 8), 8), :]
+        return rcopy(src, s.bb.at[k], s.bs.at[3, k], s.br.at[3, k], (db, p.z))
+
+    def vectors_out():
+        pack_vectors(s)
+        for k in range(1, 4):
+            zcopy(k).start()
+
+    def vectors_half():
+        total = s.pb[pl.ds(pl.multiple_of(p.z * 64, 64), 64), :]
+        for k in range(1, 4):
+            zcopy(k).wait()
+            total = total + s.zb[k]
+        s.half[...] = total
+        for k in range(1, 8):
             bcopy(k).start()
-        else:
-            s.bias_out[...] = total
+
+    def vectors_in():
+        total = s.half[pl.ds(pl.multiple_of(p.b * 8, 8), 8), :]
+        for k in range(1, 8):
+            bcopy(k).wait()
+            total = total + s.bb[k]
+        s.bias_out[...] = total
 
     def drain():
         for kind, ref in ((0, s.wa), (1, s.wb)):
@@ -1249,17 +1284,23 @@
             Scatter(p, ref, kind, sems, sems, (None,) * 6, (ALL,)).drain()
         rcopy(s.st, s.r1, s.g1s.at[0], s.g1r.at[0], p.zdev).wait_send()
 
-    return stages, query_steps, [lambda k=k: bias_step(k) for k in range(6)], drain
+    return stages, (vectors_out, vectors_half, vectors_in), early, drain
+
+
+def done_by(spans, t):
+    total = 0
+    for first, many, chunks in spans:
+        total = total + jnp.minimum(jnp.maximum((t - first + 1) * many, 0), chunks)
+    return total
+
+
+def run_span(spans, t, fn):
+    pl.loop(done_by(spans, t - 1), done_by(spans, t))(fn)
 
 
 def run_stages(stages, t):
-    for off, many, fn in stages:
-        for k in range(many):
-            ci = (t - off) * many + k
-
-            @pl.when((ci >= 0) & (ci < NC))
-            def _(ci=ci, fn=fn):
-                fn(ci)
+    for spans, fn in stages:
+        run_span(spans, t, fn)
 
 
 def run_at(t, table):
@@ -1280,6 +1321,7 @@
     me = p.b * 4 + p.z
     vectors = Spread(p, s, s.small, 0, 8)
     scores = Spread(p, s, s.sc, 1, 8)
+    firsts = Spread(p, s, s.call, 2, 16)
     copies = {
         name: pltpu.make_async_copy(src, dst, s.io.at[k])
         for k, (name, src, dst) in enumerate(
@@ -1305,59 +1347,68 @@
         vectors.finish()
         unpack_small(s)
 
-    ready = 2 * PARTS - 1 + G_END
     forward = [
         (1, copies["x"].wait),
         (1, copies["up"].wait),
         (2, vectors.second),
         (6, small_done),
-        (ready, lambda: qkv(s)),
-        (ready + 1, passages(attn_fwd, 0, 2)),
-        (ready + 2, passages(attn_fwd, 2, 2)),
-        (ready + 3, lambda: attn_out(s)),
+        (7, lambda: queries_keys(s)),
+        (9, lambda: values(s)),
+        (9, passages(attn_fwd, 0, 1)),
+        (10, passages(attn_fwd, 1, 2)),
+        (11, passages(attn_fwd, 3, 1)),
+        (11, lambda: attn_out(s)),
     ]
-    forward += [(6 + 2 * k, fn) for k, fn in enumerate(query_steps)]
-    forward += [(15, lambda: unpack_queries(s))]
-
-    def ffn_until(t):
-        return jnp.minimum(jnp.maximum(2 * (t - ready - 3), 0), jnp.maximum(t - ready, 0))
-
-    @pl.loop(0, NC + G_END)
+    forward += [(5 + 2 * k, fn) for k, fn in enumerate(query_steps)]
+    forward += [(14, lambda: unpack_queries(s))]
+
+    @pl.loop(0, G_END)
     def _(t):
         run_stages(stages, t)
         run_at(t, forward)
-        pl.loop(ffn_until(t - 1), ffn_until(t))(lambda h: ffn_fwd(s, h))
-
-    drain()
-    s.sc[pl.ds(pl.multiple_of(me * 8, 8), 8), :] = first_rows(s)
+        run_span(G_FULL, t, lambda j: ffn_fwd(s, j, 0, D))
+        run_span(G_HALF, t, lambda h: ffn_fwd(s, 3, h, LW))
+
+    s.sc[pl.ds(pl.multiple_of(me * 8, 8), 8), :] = first_rows(s, me)
     scores.first()
-    s.gv[...] = jnp.zeros_like(s.gv)
+    firsts.first()
     norm2(s)
     copies["lo"].start()
     scores.second()
+    firsts.second()
+    drain()
+    s.gv[...] = jnp.zeros_like(s.gv)
     norm2_back(s)
     scores.finish()
     loss_part(s, me)
     add_cls(s)
 
-    stages, query_steps, bias_steps, drain = scatter_steps(p, s)
-    ffn_back(s, 0)
+    stages, vector_steps, early, drain = scatter_steps(p, s)
+    outer_back(s, 0)
+    early(1)
+    inner_back(s, 0)
+    early(0)
     def hidden():
         qkv_back(s)
         copies["hg"].start()
+
+    def query():
+        firsts.finish()
+        query_gradient(s, me)
 
     backward = [
         (3, lambda: norm1_back(s)),
         (4, passages(attn_back, 0, 1)),
         (5, passages(attn_back, 1, 1)),
         (6, passages(attn_back, 2, 2)),
-        (7, hidden),
-        (8, lambda: query_rows(s)),
+        (8, hidden),
+        (9, query),
+        (10, vector_steps[0]),
+        (13, vector_steps[1]),
+        (17, vector_steps[2]),
     ]
-    backward += [(9 + k, fn) for k, fn in enumerate(query_steps)]
-    backward += [(8 + 2 * k, fn) for k, fn in enumerate(bias_steps)]
-
-    @pl.loop(0, max(S_END, 18) + 1)
+
+    @pl.loop(0, S_END)
     def _(t):
         run_stages(stages, t)
 
@@ -1389,14 +1440,19 @@
 
 
 def finish_kernel(
-    out, q_out, bias, loss, cgrad,
-    query_grad, query_loss, g_query, g_key, g_value, g_attn,
-    g_qb, g_vb, g_ab, g_fg, g_fs, g_inner, g_ib, g_outer, g_ob, g_sg, g_ss, cls_grad
+    lo_in, hg_in, out, q_out, bias, loss, cgrad,
+    lo, hg, query_grad, query_loss, g_query, g_key, g_value, g_attn,
+    g_qb, g_vb, g_ab, g_fg, g_fs, g_inner, g_ib, g_outer, g_ob, g_sg, g_ss, cls_grad, held, sems
 ):
     me = lax.axis_index("blk") * 4 + lax.axis_index("grp")
-    for q in range(4):
-        for k in range(6):
-            query_grad[q : q + 1, k * 128 : (k + 1) * 128] = q_out[6 * q + k : 6 * q + k + 1, :]
+    into = [pltpu.make_async_copy(ref, held.at[k], sems.at[k]) for k, ref in enumerate((lo_in, hg_in))]
+    away = [pltpu.make_async_copy(held.at[k], ref, sems.at[2 + k]) for k, ref in enumerate((lo, hg))]
+    for move in into:
+        move.start()
+    for k in range(2):
+        into[k].wait()
+        away[k].start()
+    query_grad[...] = q_out[0:4, :]
     cls_grad[...] = cgrad[0:4, :]
     g_query[...] = out[0, :ROWS]
     g_key[...] = out[0, ROWS:]
@@ -1406,28 +1462,27 @@
         at = slice(j * D, (j + 1) * D)
         g_inner[:, at] = out[2 + j, :ROWS]
         g_outer[:, at] = out[2 + j, ROWS:]
-    wide = pltpu.roll(bias[0:8, :], lax.rem(D - ROWS * me, D), 1)
     for t, ref in enumerate((g_qb, g_vb, g_ab, g_fg, g_fs, g_ob, g_sg, g_ss)):
-        ref[...] = wide[t, :ROWS]
-    group = me // 8
-    inner = jnp.sum(jnp.where(lax.broadcasted_iota(jnp.int32, (8, D), 0) == group, bias[8:16, :], 0.0), axis=0, keepdims=True)
-    inner = jnp.broadcast_to(inner, (8, D))
-    inner = pltpu.roll(inner, lax.rem(D - 96 * lax.rem(me, 8), D), 1)
-    g_ib[...] = inner[0, :96]
+        ref[...] = pltpu.roll(bias[...], 32, 1)[t, :ROWS]
+    g_ib[...] = bias[0, :96]
     query_loss[...] = pltpu.roll(loss[...], lax.rem(128 - 4 * me, 128), 1)[0, :4]
+    for move in away:
+        move.wait()
 
 
 def finish(*args):
     f32 = lambda *dims: jax.ShapeDtypeStruct(dims, F32)
     square = f32(ROWS, D)
     vec = f32(ROWS)
-    outs = [f32(4, D), f32(4)] + [square] * 4 + [vec] * 5
+    tokens = jax.ShapeDtypeStruct((TOK, D), BF)
+    outs = [tokens, tokens, f32(4, D), f32(4)] + [square] * 4 + [vec] * 5
     outs += [f32(ROWS, 4 * D), f32(96), f32(ROWS, 4 * D), vec, vec, vec, f32(4, D)]
     return pl.pallas_call(
         finish_kernel,
         out_shape=outs,
-        in_specs=[VM] * 5,
-        out_specs=[VM] * 18,
+        in_specs=[HBM] * 2 + [VM] * 5,
+        out_specs=[HBM] * 2 + [VM] * 18,
+        scratch_shapes=[pltpu.VMEM((2, TOK, D), BF), DMA((4,))],
         compiler_params=pltpu.CompilerParams(vmem_limit_bytes=VMEM_LIMIT),
     )(*args)
 
@@ -1478,11 +1533,10 @@
         positive_ids,
         positive_count,
     )
-    layer_output, hidden_grad = (part.reshape(hidden_in.shape) for part in results[:2])
-    rest = list(finish(*results[2:]))
+    layer_output, hidden_grad, *rest = finish(*results)
     rest[5] = rest[5].T
     rest[13] = rest[13].T
-    return (layer_output, hidden_grad, *rest)
+    return (layer_output.reshape(hidden_in.shape), hidden_grad.reshape(hidden_in.shape), *rest)
 
 
 def solution(mesh):

time: 165 us -> 156 us (0.945)
  Pallas kernels: 161 us -> 154 us
  local copies, waits for them, and re-layouts: 2.29 us -> 0 us
    pallas_call x1, Pallas kernels: 159 us -> 150 us  [layer(): pl.pallas_call(layer_kernel, out_shape=tuple((jax.ShapeDtypeStruct(*o) fo...]
    unnamed x6 -> x0, local copies, waits for them, and re-layouts: 2.29 us -> none
    pallas_call x1, Pallas kernels: 2.25 us -> 4.46 us  [finish(): pl.pallas_call(finish_kernel, out_shape=outs, in_specs=[HBM] * 2 + [VM] *...]
where the time goes in v4:
time: 156 us; the launch traced here: 155 us
  Pallas kernels  154 us (99%)
    pallas_call x1, Pallas kernels, layer(): pl.pallas_call(layer_kernel, out_shape=tuple((jax.ShapeDtypeStruct(*o) fo...  150 us
    pallas_call x1, Pallas kernels, finish(): pl.pallas_call(finish_kernel, out_shape=outs, in_specs=[HBM] * 2 + [VM] *...  4.46 us

profile of v4, /device:TPU:0, one launch (start us, length us, event | category | flops | bytes accessed | tf_op | source)
XLA Modules:
  0.0 155.3 jit_solution(8662228609777197632)
XLA Ops:
  0.7 150.0 %shard_map.356 = (bf16[512,768]{1,0:T(8,128)(2,1)}, bf16[512,768]{1,0:T(8,128)(2,1)}, f32[6,48,768]{2,1,0:T(8,128)}, f32[8,768]{1,0:T(8,128)}, f32[8,128]{1,0:T(...) custom-call(bf16[512,768]{1,0:T(8,128)(2,1)} %bitcast.8, bf16[512,768]{1,0:T(8,128)(2,1)} %bitcast.9, ...), custom_call_target="tpu_custom_call" | custom-call | tf_op jit(solution)/shard_map/pallas_call | solution.py:1430
  150.7 4.5 %shard_map.357 = (bf16[512,768]{1,0:T(8,128)(2,1)}, bf16[512,768]{1,0:T(8,128)(2,1)}, f32[4,768]{1,0:T(4,128)}, f32[4]{0:T(128)}, f32[24,768]{1,0:T(8,128)}, /*i...) custom-call(bf16[512,768]{1,0:T(8,128)(2,1)} %get-tuple-element.47.l, ...), custom_call_target="tpu_custom_call" | custom-call | tf_op jit(solution)/shard_map/pallas_call | solution.py:1480

commit v5 on v4

--- a/solution.py
+++ b/solution.py
@@ -448,23 +448,17 @@
         self.go(3, self.at(ALL, self.s, self.p.zh), self.sdev)
 
     def s4b_send(self):
-        self.go(6, self.at(ALL, self.s, 1 - self.p.zh), self.sdev)
+        self.go(4, self.at(ALL, self.s, 1 - self.p.zh), self.sdev)
 
     def s4_recv(self):
         self.got(3, self.at(ALL, 1 - self.s, self.p.zh))
-        self.got(6, self.at(ALL, 1 - self.s, 1 - self.p.zh))
-
-    def c1_send(self):
-        self.go(4, self.at(ALL, self.s, ALL), self.p.cdev)
-
-    def c1_recv(self):
-        self.got(4, self.at(ALL, self.s, ALL, 1 - self.p.c))
-
-    def c2_send(self):
-        self.go(5, self.at(ALL, 1 - self.s, ALL), self.p.cdev)
-
-    def c2_recv(self):
-        self.got(5, self.at(ALL, 1 - self.s, ALL, 1 - self.p.c))
+        self.got(4, self.at(ALL, 1 - self.s, 1 - self.p.zh))
+
+    def core_send(self):
+        self.go(5, self.at(ALL, ALL, ALL), self.p.cdev)
+
+    def core_recv(self):
+        self.got(5, self.at(ALL, ALL, ALL, 1 - self.p.c))
 
     def drain(self):
         self.sent(0, self.at(self.f, self.s, self.p.zh))
@@ -475,9 +469,8 @@
             self.sent(2, self.at(ALL, self.s, 1 - self.p.zh))
 
         self.sent(3, self.at(ALL, self.s, self.p.zh))
-        self.sent(6, self.at(ALL, self.s, 1 - self.p.zh))
-        self.sent(4, self.at(ALL, self.s, ALL))
-        self.sent(5, self.at(ALL, 1 - self.s, ALL))
+        self.sent(4, self.at(ALL, self.s, 1 - self.p.zh))
+        self.sent(5, self.at(ALL, ALL, ALL))
 
 
 def lanes_of(ci):
@@ -906,7 +899,7 @@
 OUTS = dict(
     lo_out=((TOK, D), BF),
     hg_out=((TOK, D), BF),
-    out=((6, 48, D), F32),
+    sums_out=((6, 48, D), F32),
     q_out=((8, D), F32),
     bias_out=((8, 128), F32),
     loss=((8, 128), F32),
@@ -935,6 +928,7 @@
     up=((TOK, D), BF),
     lo=((TOK, D), BF),
     hg=((TOK, D), BF),
+    out=((6, 48, D), F32),
     q=((TOK, D), BF),
     k=((TOK, D), BF),
     v=((TOK, D), BF),
@@ -978,17 +972,17 @@
     half=((64, 128), F32),
 )
 SEMS = dict(
-    gs=(7, 2),
-    gr=(7, 2, NC),
+    gs=(6, 2),
+    gr=(6, 2, NC),
     g1s=(1,),
     g1r=(NC,),
     xs=(8,),
     xr=(8,),
-    zs=(4, 4),
-    zr=(4, 4),
-    bs=(4, 8),
-    br=(4, 8),
-    io=(4,),
+    zs=(3, 4),
+    zr=(3, 4),
+    bs=(3, 8),
+    br=(3, 8),
+    io=(5,),
 )
 
 
@@ -1092,17 +1086,15 @@
 
         for f in fs:
             f.s4b_send()
-            f.c1_send()
 
     def s45(fs):
         for f in fs:
             f.s4_recv()
-            f.c2_send()
+            f.core_send()
 
     def core(fs):
         for f in fs:
-            f.c1_recv()
-            f.c2_recv()
+            f.core_recv()
 
     def drain():
         for kind, ref in ((0, s.wa), (1, s.wb)):
@@ -1111,16 +1103,16 @@
         rcopy(s.pack, s.rb, s.g1s.at[0], s.g1r.at[0], p.zdev).wait_send()
         q.drain()
 
+    q = Gather(p, s.qx, 0, lambda st: s.xs.at[st], lambda st: s.xr.at[st])
+    q1 = rcopy(s.qpack, s.qrb, s.xs.at[7], s.xr.at[7], p.zdev)
     for i in range(6):
         pack_weights(s, i)
         for h in range(PARTS):
             s1(PARTS * i + h).start()
-
-    s.small[pl.ds(pl.multiple_of(me * 8, 8), 8), :] = pack_small(s)
-    vectors.first()
-    q = Gather(p, s.qx, 0, lambda st: s.xs.at[st], lambda st: s.xr.at[st])
-    q1 = rcopy(s.qpack, s.qrb, s.xs.at[7], s.xr.at[7], p.zdev)
-    q1.start()
+        if i == 0:
+            s.small[pl.ds(pl.multiple_of(me * 8, 8), 8), :] = pack_small(s)
+            vectors.first()
+            q1.start()
 
     def qmerge():
         q1.wait()
@@ -1233,6 +1225,7 @@
         s1(ci).wait_recv()
         at = (piece(ci), ALL, lanes_of(ci))
         s.out[at] = s.out[at] + s.r1[ci].astype(F32)
+        pltpu.make_async_copy(s.out.at[at], s.sums_out.at[at], s.io.at[4]).start()
 
     def pack_of(fn):
         return lambda ci: fn(flows(ci))
@@ -1250,12 +1243,12 @@
     def zcopy(k):
         dz = (p.z + k) % 4
         src = s.pb.at[pl.ds(pl.multiple_of(dz * 64, 64), 64), :]
-        return rcopy(src, s.zb.at[k], s.zs.at[3, k], s.zr.at[3, k], (p.b, dz))
+        return rcopy(src, s.zb.at[k], s.zs.at[0, k], s.zr.at[0, k], (p.b, dz))
 
     def bcopy(k):
         db = (p.b + k) % 8
         src = s.half.at[pl.ds(pl.multiple_of(db * 8, 8), 8), :]
-        return rcopy(src, s.bb.at[k], s.bs.at[3, k], s.br.at[3, k], (db, p.z))
+        return rcopy(src, s.bb.at[k], s.bs.at[0, k], s.br.at[0, k], (db, p.z))
 
     def vectors_out():
         pack_vectors(s)
@@ -1371,14 +1364,13 @@
 
     s.sc[pl.ds(pl.multiple_of(me * 8, 8), 8), :] = first_rows(s, me)
     scores.first()
+    s.gv[...] = jnp.zeros_like(s.gv)
+    norm2(s)
+    norm2_back(s)
+    scores.second()
     firsts.first()
-    norm2(s)
     copies["lo"].start()
-    scores.second()
-    firsts.second()
     drain()
-    s.gv[...] = jnp.zeros_like(s.gv)
-    norm2_back(s)
     scores.finish()
     loss_part(s, me)
     add_cls(s)
@@ -1397,6 +1389,7 @@
         query_gradient(s, me)
 
     backward = [
+        (1, firsts.second),
         (3, lambda: norm1_back(s)),
         (4, passages(attn_back, 0, 1)),
         (5, passages(attn_back, 1, 1)),
@@ -1421,6 +1414,7 @@
     drain()
     copies["lo"].wait()
     copies["hg"].wait()
+    pltpu.make_async_copy(s.out, s.sums_out, s.io.at[4]).wait()
 
 
 SMEM = pl.BlockSpec(memory_space=pltpu.SMEM)
@@ -1431,7 +1425,7 @@
         layer_kernel,
         out_shape=tuple(jax.ShapeDtypeStruct(*o) for o in OUTS.values()),
         in_specs=[HBM] * 2 + [VM] * (len(INS) - 5) + [SMEM] * 3,
-        out_specs=(HBM,) * 2 + (VM,) * 5,
+        out_specs=(HBM,) * 3 + (VM,) * 4,
         scratch_shapes=[pltpu.VMEM(*b) for b in SCRATCH.values()] + [DMA(n) for n in SEMS.values()],
         compiler_params=pltpu.CompilerParams(
             collective_id=1, has_side_effects=True, vmem_limit_bytes=VMEM_LIMIT
@@ -1442,26 +1436,36 @@
 def finish_kernel(
     lo_in, hg_in, out, q_out, bias, loss, cgrad,
     lo, hg, query_grad, query_loss, g_query, g_key, g_value, g_attn,
-    g_qb, g_vb, g_ab, g_fg, g_fs, g_inner, g_ib, g_outer, g_ob, g_sg, g_ss, cls_grad, held, sems
+    g_qb, g_vb, g_ab, g_fg, g_fs, g_inner, g_ib, g_outer, g_ob, g_sg, g_ss, cls_grad, held, sums, sems
 ):
     me = lax.axis_index("blk") * 4 + lax.axis_index("grp")
-    into = [pltpu.make_async_copy(ref, held.at[k], sems.at[k]) for k, ref in enumerate((lo_in, hg_in))]
-    away = [pltpu.make_async_copy(held.at[k], ref, sems.at[2 + k]) for k, ref in enumerate((lo, hg))]
+    part = TOK // 8
+    into, away = [], []
+    for k, (src, dst) in enumerate(((lo_in, lo), (hg_in, hg))):
+        for h in range(8):
+            at = pl.ds(h * part, part)
+            into.append(pltpu.make_async_copy(src.at[at], held.at[k, at], sems.at[0, 8 * k + h]))
+            away.append(pltpu.make_async_copy(held.at[k, at], dst.at[at], sems.at[1, 8 * k + h]))
+    top, low = pl.ds(0, ROWS), pl.ds(ROWS, ROWS)
+    pieces = [(0, top, g_query), (0, low, g_key), (1, top, g_value), (1, low, g_attn)]
+    for j in range(4):
+        at = pl.ds(j * D, D)
+        pieces += [(2 + j, top, g_inner.at[:, at]), (2 + j, low, g_outer.at[:, at])]
+    for i in range(6):
+        into.append(pltpu.make_async_copy(out.at[i], sums.at[i], sems.at[0, 16 + i]))
+    for n, (i, rows, dst) in enumerate(pieces):
+        away.append(pltpu.make_async_copy(sums.at[i, rows], dst, sems.at[1, 16 + n]))
     for move in into:
         move.start()
-    for k in range(2):
+    for k in range(16):
         into[k].wait()
         away[k].start()
+    for i in range(6):
+        into[16 + i].wait()
+    for n in range(12):
+        away[16 + n].start()
     query_grad[...] = q_out[0:4, :]
     cls_grad[...] = cgrad[0:4, :]
-    g_query[...] = out[0, :ROWS]
-    g_key[...] = out[0, ROWS:]
-    g_value[...] = out[1, :ROWS]
-    g_attn[...] = out[1, ROWS:]
-    for j in range(4):
-        at = slice(j * D, (j + 1) * D)
-        g_inner[:, at] = out[2 + j, :ROWS]
-        g_outer[:, at] = out[2 + j, ROWS:]
     for t, ref in enumerate((g_qb, g_vb, g_ab, g_fg, g_fs, g_ob, g_sg, g_ss)):
         ref[...] = pltpu.roll(bias[...], 32, 1)[t, :ROWS]
     g_ib[...] = bias[0, :96]
@@ -1480,9 +1484,9 @@
     return pl.pallas_call(
         finish_kernel,
         out_shape=outs,
-        in_specs=[HBM] * 2 + [VM] * 5,
-        out_specs=[HBM] * 2 + [VM] * 18,
-        scratch_shapes=[pltpu.VMEM((2, TOK, D), BF), DMA((4,))],
+        in_specs=[HBM] * 3 + [VM] * 4,
+        out_specs=[HBM] * 2 + [VM] * 2 + [HBM] * 4 + [VM] * 5 + [HBM, VM, HBM] + [VM] * 4,
+        scratch_shapes=[pltpu.VMEM((2, TOK, D), BF), pltpu.VMEM((6, 48, D), F32), DMA((2, 28))],
         compiler_params=pltpu.CompilerParams(vmem_limit_bytes=VMEM_LIMIT),
     )(*args)
 

time: 156 us -> 152 us (0.974)
  Pallas kernels: 154 us -> 151 us
    pallas_call x1, Pallas kernels: 150 us -> 146 us  [layer(): pl.pallas_call(layer_kernel, out_shape=tuple((jax.ShapeDtypeStruct(*o) fo...]
where the time goes in v5:
time: 152 us; the launch traced here: 151 us
  Pallas kernels  151 us (99%)
    pallas_call x1, Pallas kernels, layer(): pl.pallas_call(layer_kernel, out_shape=tuple((jax.ShapeDtypeStruct(*o) fo...  146 us
    pallas_call x1, Pallas kernels, finish(): pl.pallas_call(finish_kernel, out_shape=outs, in_specs=[HBM] * 3 + [VM] *...  4.54 us

profile of v5, /device:TPU:0, one launch (start us, length us, event | category | flops | bytes accessed | tf_op | source)
XLA Modules:
  0.0 151.4 jit_solution(4764064282562967748)
XLA Ops:
  0.7 146.0 %shard_map.356 = (bf16[512,768]{1,0:T(8,128)(2,1)}, bf16[512,768]{1,0:T(8,128)(2,1)}, f32[6,48,768]{2,1,0:T(8,128)}, f32[8,768]{1,0:T(8,128)}, f32[8,128]{1,0:T(...) custom-call(bf16[512,768]{1,0:T(8,128)(2,1)} %bitcast.8, bf16[512,768]{1,0:T(8,128)(2,1)} %bitcast.9, ...), custom_call_target="tpu_custom_call" | custom-call | tf_op jit(solution)/shard_map/pallas_call | solution.py:1424
  146.7 4.5 %shard_map.357 = (bf16[512,768]{1,0:T(8,128)(2,1)}, bf16[512,768]{1,0:T(8,128)(2,1)}, f32[4,768]{1,0:T(4,128)}, f32[4]{0:T(128)}, f32[24,768]{1,0:T(8,128)}, /*i...) custom-call(bf16[512,768]{1,0:T(8,128)(2,1)} %get-tuple-element.47.l, ...), custom_call_target="tpu_custom_call" | custom-call | tf_op jit(solution)/shard_map/pallas_call | solution.py:1484

commit v6 on v5

--- a/solution.py
+++ b/solution.py
@@ -1396,9 +1396,9 @@
         (6, passages(attn_back, 2, 2)),
         (8, hidden),
         (9, query),
-        (10, vector_steps[0]),
-        (13, vector_steps[1]),
-        (17, vector_steps[2]),
+        (9, vector_steps[0]),
+        (12, vector_steps[1]),
+        (18, vector_steps[2]),
     ]
 
     @pl.loop(0, S_END)

time: 152 us -> 152 us (level)
  no operation moved by 1% of the time
where the time goes in v6:
time: 152 us; the launch traced here: 151 us
  Pallas kernels  150 us (99%)
    pallas_call x1, Pallas kernels, layer(): pl.pallas_call(layer_kernel, out_shape=tuple((jax.ShapeDtypeStruct(*o) fo...  146 us
    pallas_call x1, Pallas kernels, finish(): pl.pallas_call(finish_kernel, out_shape=outs, in_specs=[HBM] * 3 + [VM] *...  4.54 us

profile of v6, /device:TPU:0, one launch (start us, length us, event | category | flops | bytes accessed | tf_op | source)
XLA Modules:
  0.0 151.3 jit_solution(10331022587992501304)
XLA Ops:
  0.7 145.9 %shard_map.356 = (bf16[512,768]{1,0:T(8,128)(2,1)}, bf16[512,768]{1,0:T(8,128)(2,1)}, f32[6,48,768]{2,1,0:T(8,128)}, f32[8,768]{1,0:T(8,128)}, f32[8,128]{1,0:T(...) custom-call(bf16[512,768]{1,0:T(8,128)(2,1)} %bitcast.8, bf16[512,768]{1,0:T(8,128)(2,1)} %bitcast.9, ...), custom_call_target="tpu_custom_call" | custom-call | tf_op jit(solution)/shard_map/pallas_call | solution.py:1424
  146.6 4.5 %shard_map.357 = (bf16[512,768]{1,0:T(8,128)(2,1)}, bf16[512,768]{1,0:T(8,128)(2,1)}, f32[4,768]{1,0:T(4,128)}, f32[4]{0:T(128)}, f32[24,768]{1,0:T(8,128)}, /*i...) custom-call(bf16[512,768]{1,0:T(8,128)(2,1)} %get-tuple-element.47.l, ...), custom_call_target="tpu_custom_call" | custom-call | tf_op jit(solution)/shard_map/pallas_call | solution.py:1484
